TPU v7x, 32 devices: a whole 2x2x4 slice. The times are simulated.
32 devices in a mesh: expert: 8 (over z, core), shard: 4 (over y, x).
Axes of the slice: x: 2, y: 2, z: 4, core: 2. Of those that a mesh axis runs over, the one named last changes fastest.
Arguments:
- tokens: bfloat16 [8192, 768], P(('expert', 'shard')), may hold values from -6 to 6
- segments: int32 [8192], P(('expert', 'shard')), may hold values from 0 to 2, as said below
- routes: int32 [8192, 1], P(('expert', 'shard')), may hold values from 0 to 7; in each aligned block of 256 rows (0 to 255, 256 to 511, ...) at most 64 rows name the same one
- buckets: int32 [2047], replicated, may hold values from 0 to 31
- gain_attn: float32 [768], replicated, may hold values from 0.5 to 1.5
- gain_moe: float32 [768], replicated, may hold values from 0.5 to 1.5
- rel_table: float32 [32, 12], replicated, may hold values from -6 to 6
- router_weight: float32 [768, 8], replicated, may hold values from -0.111 to 0.111
- qkv_weight: bfloat16 [768, 2304], P('shard'), may hold values from -0.21875 to 0.21875
- out_weight: bfloat16 [768, 768], P('shard'), may hold values from -3.5 to 3.5
- w_in: bfloat16 [8, 768, 3072], P('expert', 'shard'), may hold values from -0.21875 to 0.21875
- w_out: bfloat16 [8, 3072, 768], P('expert', 'shard'), may hold values from -0.875 to 0.875
- out_grad: bfloat16 [8192, 768], P(('expert', 'shard')), may hold values from -6 to 6
Outputs:
- output: bfloat16 [8192, 768], P(('expert', 'shard'))
- grad_tokens: float32 [8192, 768], P(('expert', 'shard'))
- grad_gain_attn: float32 [768], replicated
- grad_gain_moe: float32 [768], replicated
- grad_rel_table: float32 [32, 12], replicated
- grad_router: float32 [768, 8], replicated
- grad_qkv_weight: float32 [768, 2304], P('shard')
- grad_out_weight: float32 [768, 768], P('shard')
- grad_w_in: float32 [8, 768, 3072], P('expert', 'shard')
- grad_w_out: float32 [8, 3072, 768], P('expert', 'shard')
Inputs may be any that keep to these rules, and one draw needn't show every extreme that they name: `segments`: within each sequence of 1024 tokens the numbers are 0, 1, 2 in order, each present; number 1 begins within the sequence's first 256 tokens and number 2 within its last 256. `routes`: in each aligned block of 256 rows (the rows of one device) no expert is named by more than 64 rows, a bound that some block reaches.
All inputs are finite; a program needn't handle non-finite values.
Results may differ from a plain program's by a relative error of at most 0.03.
Values may be sent and summed in bfloat16 or wider, within the bound.
A program may use at most 192 MiB of HBM per device.

v0:
```python
from functools import partial

import jax
import jax.numpy as jnp
from jax import lax
from jax.sharding import PartitionSpec as P

epsilon = 1e-06
neg_large = -1000000000.0
highest = lax.Precision.HIGHEST


def norm_rows(values, gain):
    inverse = lax.rsqrt(jnp.mean(values * values, axis=1, keepdims=True) + epsilon)
    return (values * inverse * gain, inverse)


def norm_back(values, inverse, gain, upstream):
    scaled = upstream * gain
    gain_grad = jnp.sum(upstream * values * inverse, axis=0)
    input_grad = inverse * scaled - values * inverse**3 * jnp.mean(
        scaled * values, axis=1, keepdims=True
    )
    return (input_grad, gain_grad)


def contract_rows(left, right, precision_level=None):
    return lax.dot_general(
        left,
        right,
        (((0,), (0,)), ((), ())),
        precision=precision_level,
        preferred_element_type=jnp.float32,
    )


def by_blocks(update, running, pieces):
    total_rows = pieces[0].shape[0]
    block_rows = 512

    def advance(block_index, state):
        parts = tuple(
            (
                lax.dynamic_slice_in_dim(member, block_index * block_rows, block_rows, 0)
                for member in pieces
            )
        )
        return update(state, parts, block_index * block_rows)

    return lax.fori_loop(0, total_rows // block_rows, advance, running)


def body(
    tokens,
    segments,
    routes,
    buckets,
    gain_attn,
    gain_moe,
    rel_table,
    router_weight,
    qkv_weight,
    out_weight,
    w_in,
    w_out,
    out_grad,
):
    rows_here = tokens.shape[0]
    width = tokens.shape[1]
    heads = rel_table.shape[1]
    head_size = width // heads
    span = buckets.shape[0]
    experts = router_weight.shape[1]
    capacity = 2 * rows_here // experts
    score_scale = head_size ** (-0.5)
    shard_count = lax.axis_size("shard")
    query_base = lax.axis_index("shard") * rows_here
    qkv_full, out_full = (
        lax.all_gather(qkv_weight, "shard", axis=0, tiled=True),
        lax.all_gather(out_weight, "shard", axis=0, tiled=True),
    )
    in_full, out_ff_full = (
        lax.all_gather(w_in[0], "shard", axis=0, tiled=True),
        lax.all_gather(w_out[0], "shard", axis=0, tiled=True),
    )
    inputs32 = tokens.astype(jnp.float32)
    normed_attn, inverse_attn = norm_rows(inputs32, gain_attn)
    normed_attn_b = normed_attn.astype(jnp.bfloat16)
    qkv_b = jnp.dot(normed_attn_b, qkv_full, preferred_element_type=jnp.float32).astype(
        jnp.bfloat16
    )
    queries = qkv_b[:, :width].reshape(rows_here, heads, head_size)
    key_value = qkv_b[:, width:]
    bucket_onehot = jax.nn.one_hot(buckets, rel_table.shape[0], dtype=jnp.float32)
    offsets_t = jnp.dot(
        bucket_onehot, rel_table, precision=highest, preferred_element_type=jnp.float32
    ).T
    offsets_pad = jnp.concatenate([offsets_t, jnp.zeros((heads, 1), jnp.float32)], axis=1)

    def window_start(query_first, query_count, key_first):
        return key_first - query_first - (query_count - 1) + span // 2

    def bias_block(query_first, query_count, key_first, key_count):
        total = query_count + key_count
        window = lax.dynamic_slice_in_dim(
            offsets_pad, window_start(query_first, query_count, key_first), total, 1
        )
        tiled = jnp.tile(window, (1, query_count))
        cut = tiled[:, query_count - 1 : query_count - 1 + query_count * (total - 1)]
        return cut.reshape(heads, query_count, total - 1)[:, :, :key_count]

    def bias_back(grid_grad):
        query_count = grid_grad.shape[1]
        key_count = grid_grad.shape[2]
        total = query_count + key_count
        widened = jnp.pad(grid_grad, ((0, 0), (0, 0), (0, total - 1 - key_count)))
        flat = widened.reshape(heads, query_count * (total - 1))
        flat = jnp.pad(flat, ((0, 0), (query_count - 1, 1)))
        return jnp.sum(flat.reshape(heads, query_count, total), axis=1)

    def add_window(bias_total, summed, start):
        current = lax.dynamic_slice_in_dim(bias_total, start, summed.shape[1], 1)
        return lax.dynamic_update_slice_in_dim(bias_total, current + summed, start, 1)

    def pair_scores(query_part, query_first, query_seg, key_part, key_first, key_seg):
        products = (
            jnp.einsum("qhd,khd->hqk", query_part, key_part, preferred_element_type=jnp.float32)
            * score_scale
        )
        allowed = (query_seg[:, None] == key_seg[None, :])[None]
        bias = bias_block(query_first, query_part.shape[0], key_first, key_part.shape[0])
        return (products + bias, allowed)

    def split_pairs(kv_piece):
        length = kv_piece.shape[0]
        key_part = kv_piece[:, :width].reshape(length, heads, head_size)
        value_part = kv_piece[:, width:].reshape(length, heads, head_size)
        return (key_part, value_part)

    def forward_step(running, pieces, first_row):
        running_max, running_sum, accum = running
        kv_piece, seg_piece = pieces
        key_part, value_part = split_pairs(kv_piece)
        scores, allowed = pair_scores(queries, query_base, segments, key_part, first_row, seg_piece)
        masked = jnp.where(allowed, scores, neg_large)
        new_max = jnp.maximum(running_max, jnp.max(masked, axis=2))
        weights = jnp.where(allowed, jnp.exp(masked - new_max[:, :, None]), 0.0)
        factor = jnp.exp(running_max - new_max)
        new_sum = running_sum * factor + jnp.sum(weights, axis=2)
        increment = jnp.einsum(
            "hqk,khd->hqd",
            weights.astype(jnp.bfloat16),
            value_part,
            preferred_element_type=jnp.float32,
        )
        return (new_max, new_sum, accum * factor[:, :, None] + increment)

    start_state = (
        jnp.full((heads, rows_here), neg_large, jnp.float32),
        jnp.zeros((heads, rows_here), jnp.float32),
        jnp.zeros((heads, rows_here, head_size), jnp.float32),
    )
    final_max, final_sum, final_accum = by_blocks(
        forward_step,
        start_state,
        (
            lax.all_gather(key_value, "shard", axis=0, tiled=True),
            lax.all_gather(segments, "shard", axis=0, tiled=True),
        ),
    )
    attended32 = (final_accum / final_sum[:, :, None]).transpose(1, 0, 2).reshape(rows_here, width)
    log_rows = (final_max + jnp.log(final_sum)).T
    attended_b = attended32.astype(jnp.bfloat16)
    hidden1 = inputs32 + jnp.dot(attended_b, out_full, preferred_element_type=jnp.float32)
    normed_moe, inverse_moe = norm_rows(hidden1, gain_moe)
    logits = jnp.dot(
        normed_moe, router_weight, precision=highest, preferred_element_type=jnp.float32
    )
    router_probs = jax.nn.softmax(logits, axis=1)
    route = routes[:, 0]
    route_onehot = (route[:, None] == jnp.arange(experts, dtype=jnp.int32)[None, :]).astype(
        jnp.float32
    )
    gate = jnp.sum(router_probs * route_onehot, axis=1)
    onehot_count = route_onehot.astype(jnp.int32)
    rank_in_expert = jnp.sum((jnp.cumsum(onehot_count, axis=0) - 1) * onehot_count, axis=1)
    slot_id = route * capacity + rank_in_expert
    dispatch = (
        jnp.arange(experts * capacity, dtype=jnp.int32)[:, None] == slot_id[None, :]
    ).astype(jnp.bfloat16)
    send_rows = jnp.dot(
        dispatch, normed_moe.astype(jnp.bfloat16), preferred_element_type=jnp.float32
    ).astype(jnp.bfloat16)
    send_rows = send_rows.reshape(experts, capacity, width)
    received = lax.all_to_all(send_rows, "expert", split_axis=0, concat_axis=0, tiled=True)
    sources = received.shape[0]
    item_count = received.shape[1]
    pre = jnp.dot(received.reshape(-1, width), in_full, preferred_element_type=jnp.float32)
    hidden_ff = jax.nn.gelu(pre, approximate=False).astype(jnp.bfloat16)
    result = jnp.dot(hidden_ff, out_ff_full, preferred_element_type=jnp.float32).astype(
        jnp.bfloat16
    )
    returned_rows = lax.all_to_all(
        result.reshape(sources, item_count, width),
        "expert",
        split_axis=0,
        concat_axis=0,
        tiled=True,
    )
    pre_kept = pre.reshape(sources, item_count, -1)
    expert_out = contract_rows(dispatch, returned_rows.reshape(-1, width))
    output = (hidden1 + gate[:, None] * expert_out).astype(jnp.bfloat16)
    upstream = out_grad.astype(jnp.float32)
    gate_grad = jnp.sum(upstream * expert_out, axis=1)
    grad_slots = jnp.dot(
        dispatch,
        (gate[:, None] * upstream).astype(jnp.bfloat16),
        preferred_element_type=jnp.float32,
    ).astype(jnp.bfloat16)
    grad_received = lax.all_to_all(
        grad_slots.reshape(experts, capacity, width),
        "expert",
        split_axis=0,
        concat_axis=0,
        tiled=True,
    )
    grad_flat = grad_received.reshape(-1, width)
    pre_flat = pre_kept.reshape(grad_flat.shape[0], -1)
    hidden_ff, gelu_back = jax.vjp(partial(jax.nn.gelu, approximate=False), pre_flat)
    hidden_b = hidden_ff.astype(jnp.bfloat16)
    grad_hidden = lax.dot_general(
        grad_flat, out_ff_full, (((1,), (1,)), ((), ())), preferred_element_type=jnp.float32
    )
    grad_pre = gelu_back(grad_hidden)[0].astype(jnp.bfloat16)
    grad_back_rows = lax.dot_general(
        grad_pre, in_full, (((1,), (1,)), ((), ())), preferred_element_type=jnp.float32
    ).astype(jnp.bfloat16)
    returned_grad = lax.all_to_all(
        grad_back_rows.reshape(grad_received.shape),
        "expert",
        split_axis=0,
        concat_axis=0,
        tiled=True,
    )
    grad_in_part = contract_rows(received.reshape(-1, width), grad_pre)
    grad_out_part = contract_rows(hidden_b, grad_flat)
    grad_in_rows, grad_out_rows = (
        lax.psum_scatter(
            grad_in_part.astype(jnp.bfloat16), "shard", scatter_dimension=0, tiled=True
        ).astype(jnp.float32),
        lax.psum_scatter(
            grad_out_part.astype(jnp.bfloat16), "shard", scatter_dimension=0, tiled=True
        ).astype(jnp.float32),
    )
    grad_expert_in = contract_rows(dispatch, returned_grad.reshape(-1, width))
    logit_grad = gate_grad[:, None] * router_probs * (route_onehot - gate[:, None])
    router_grad = contract_rows(normed_moe, logit_grad, highest)
    grad_normed_moe = grad_expert_in + lax.dot_general(
        logit_grad,
        router_weight,
        (((1,), (1,)), ((), ())),
        precision=highest,
        preferred_element_type=jnp.float32,
    )
    grad_moe_in, gain_moe_grad = norm_back(hidden1, inverse_moe, gain_moe, grad_normed_moe)
    grad_hidden1 = upstream + grad_moe_in
    branch_grad = grad_hidden1.astype(jnp.bfloat16)
    grad_attended = lax.dot_general(
        branch_grad, out_full, (((1,), (1,)), ((), ())), preferred_element_type=jnp.float32
    ).astype(jnp.bfloat16)
    grad_heads = grad_attended.reshape(rows_here, heads, head_size)
    delta_rows = jnp.sum(
        grad_heads.astype(jnp.float32) * attended32.reshape(rows_here, heads, head_size), axis=2
    )

    def backward_pair(
        query_part,
        grad_part,
        log_part,
        delta_part,
        query_first,
        query_seg,
        key_part,
        value_part,
        key_first,
        key_seg,
    ):
        scores, allowed = pair_scores(
            query_part, query_first, query_seg, key_part, key_first, key_seg
        )
        weights = jnp.where(allowed, jnp.exp(scores - log_part.T[:, :, None]), 0.0)
        weight_grad = jnp.einsum(
            "qhd,khd->hqk", grad_part, value_part, preferred_element_type=jnp.float32
        )
        score_grad = (weights * (weight_grad - delta_part.T[:, :, None])).astype(jnp.bfloat16)
        query_grad = None
        key_grad = None
        value_grad = None
        bias_grad = None
        query_grad = (
            jnp.einsum("hqk,khd->qhd", score_grad, key_part, preferred_element_type=jnp.float32)
            * score_scale
        )
        key_grad = (
            jnp.einsum("hqk,qhd->khd", score_grad, query_part, preferred_element_type=jnp.float32)
            * score_scale
        )
        value_grad = jnp.einsum(
            "hqk,qhd->khd",
            weights.astype(jnp.bfloat16),
            grad_part,
            preferred_element_type=jnp.float32,
        )
        bias_grad = bias_back(score_grad.astype(jnp.float32))
        return (query_grad, key_grad, value_grad, bias_grad)

    def partial_step(running, pieces, first_row):
        query_total, key_total, bias_total = running
        kv_piece, seg_piece = pieces
        length = kv_piece.shape[0]
        key_part, value_part = split_pairs(kv_piece)
        query_grad, key_grad, value_grad, bias_grad = backward_pair(
            queries,
            grad_heads,
            log_rows,
            delta_rows,
            query_base,
            segments,
            key_part,
            value_part,
            first_row,
            seg_piece,
        )
        joined = jnp.concatenate(
            [key_grad.reshape(length, width), value_grad.reshape(length, width)], axis=1
        )
        current = lax.dynamic_slice_in_dim(key_total, first_row, length, 0)
        key_total = lax.dynamic_update_slice_in_dim(key_total, current + joined, first_row, 0)
        bias_total = add_window(
            bias_total, bias_grad, window_start(query_base, rows_here, first_row)
        )
        return (query_total + query_grad, key_total, bias_total)

    start_back = (
        jnp.zeros((rows_here, heads, head_size), jnp.float32),
        jnp.zeros((shard_count * rows_here, 2 * width), jnp.float32),
        jnp.zeros((heads, span + 1), jnp.float32),
    )
    query_total, key_all, bias_total = by_blocks(
        partial_step,
        start_back,
        (
            lax.all_gather(key_value, "shard", axis=0, tiled=True),
            lax.all_gather(segments, "shard", axis=0, tiled=True),
        ),
    )
    kv_grad = lax.psum_scatter(
        key_all.astype(jnp.bfloat16), "shard", scatter_dimension=0, tiled=True
    ).astype(jnp.float32)
    grad_qkv_b = jnp.concatenate([query_total.reshape(rows_here, width), kv_grad], axis=1).astype(
        jnp.bfloat16
    )
    grad_normed_attn = lax.dot_general(
        grad_qkv_b, qkv_full, (((1,), (1,)), ((), ())), preferred_element_type=jnp.float32
    )
    grad_attn_in, gain_attn_grad = norm_back(inputs32, inverse_attn, gain_attn, grad_normed_attn)
    grad_tokens = grad_hidden1 + grad_attn_in
    weight_rows = lax.psum_scatter(
        jnp.concatenate(
            [contract_rows(normed_attn_b, grad_qkv_b), contract_rows(attended_b, branch_grad)],
            axis=1,
        ).astype(jnp.bfloat16),
        "shard",
        scatter_dimension=0,
        tiled=True,
    ).astype(jnp.float32)
    weight_rows = lax.psum(weight_rows.astype(jnp.bfloat16), "expert").astype(jnp.float32)
    table_grad = contract_rows(bucket_onehot, bias_total[:, :span].T, highest)
    gain_attn_total, gain_moe_total, table_total, router_total = lax.psum(
        (gain_attn_grad, gain_moe_grad, table_grad, router_grad), ("expert", "shard")
    )
    return (
        output,
        grad_tokens,
        gain_attn_total,
        gain_moe_total,
        table_total,
        router_total,
        weight_rows[:, : 3 * width],
        weight_rows[:, 3 * width :],
        grad_in_rows[None],
        grad_out_rows[None],
    )


def solution(mesh):
    in_specs = (
        P(("expert", "shard"), None),
        P(("expert", "shard")),
        P(("expert", "shard"), None),
        P(),
        P(),
        P(),
        P(),
        P(),
        P("shard", None),
        P("shard", None),
        P("expert", "shard", None),
        P("expert", "shard", None),
        P(("expert", "shard"), None),
    )
    out_specs = (
        P(("expert", "shard"), None),
        P(("expert", "shard"), None),
        P(),
        P(),
        P(),
        P(),
        P("shard", None),
        P("shard", None),
        P("expert", "shard", None),
        P("expert", "shard", None),
    )
    return jax.shard_map(body, mesh=mesh, in_specs=in_specs, out_specs=out_specs, check_vma=False)
```

profile of v0, /device:TPU:0, one launch (start us, length us, event | category | flops | bytes accessed | tf_op | source)
XLA Modules:
  0.0 1009.9 jit_solution(3068839340680436633)
XLA Ops:
  9.8 50.1 %all-gather.9.cloned.1.call-done = bf16[768,2304]{1,0:T(8,128)(2,1)} async-done(((bf16[192,2304]{1,0:T(8,128)(2,1)}), bf16[768,2304]{1,0:T(8,128)(2,1)}) %all-gather.9.cloned.1.call-update) | async-done | bytes 3538960 | tf_op jit(solution)/shard_map/all_gather | solution.py:79
  66.1 8.0 all-gather.2
  77.5 30.8 %all-gather.11.cloned.1.call-done = bf16[1024,1536]{1,0:T(8,128)(2,1)} async-done(((bf16[256,1536]{1,0:T(8,128)(2,1)}), bf16[1024,1536]{1,0:T(8,128)(2,1)}) %all-gather.11.cloned.1.call-update) | async-done | bytes 3145744 | tf_op jit(solution)/shard_map/all_gather | solution.py:167
  111.5 171.0 %while.44 = (s32[]{:T(128)}, f32[12,256]{1,0:T(8,128)S(1)}, f32[12,256]{1,0:T(8,128)S(1)}, f32[12,256,64]{1,2,0:T(8,128)}, s32[256]{0:T(256)S(1)}, /*index=5*/s3...) while((s32[]{:T(128)}, f32[12,256]{1,0:T(8,128)S(1)}, ...), condition=%wide.region_4.5_spmd.clone, body=%wide.region_1.4_spmd.clone.sunk | while | flops 419118080 | bytes 161615264 | solution.py:50
  136.0 16.4 %copy.75 = f32[2,8,256,768]{3,1,2,0:T(8,128)} copy(f32[2,8,256,768]{3,2,1,0:T(8,128)} %bitcast.178) | data formatting | bytes 25165824 | tf_op jit(solution)/shard_map/while
  152.4 11.6 %slice.159 = f32[12,196352]{1,0:T(8,128)} slice(f32[12,196608]{1,0:T(8,128)} %bitcast.181), slice={[0:12], [255:196607]} | slice | bytes 18849792 | tf_op jit(solution)/shard_map/while/body/eval_jaxpr/slice | solution.py:109
  164.0 20.0 %reshape.364 = f32[12,256,767]{2,1,0:T(8,128)} reshape(f32[12,196352]{1,0:T(8,128)} %slice.159) | data formatting | bytes 18849792 | tf_op jit(solution)/shard_map/while/body/eval_jaxpr/reshape | solution.py:110
  212.8 16.8 %copy.75 = f32[2,8,256,768]{3,1,2,0:T(8,128)} copy(f32[2,8,256,768]{3,2,1,0:T(8,128)} %bitcast.178) | data formatting | bytes 25165824 | tf_op jit(solution)/shard_map/while
  229.6 11.6 %slice.159 = f32[12,196352]{1,0:T(8,128)} slice(f32[12,196608]{1,0:T(8,128)} %bitcast.181), slice={[0:12], [255:196607]} | slice | bytes 18849792 | tf_op jit(solution)/shard_map/while/body/eval_jaxpr/slice | solution.py:109
  241.2 20.0 %reshape.364 = f32[12,256,767]{2,1,0:T(8,128)} reshape(f32[12,196352]{1,0:T(8,128)} %slice.159) | data formatting | bytes 18849792 | tf_op jit(solution)/shard_map/while/body/eval_jaxpr/reshape | solution.py:110
  297.8 16.7 %all-to-all-done = bf16[8,64,768]{2,1,0:T(8,128)(2,1)} async-done(((bf16[8,64,768]{2,1,0:T(8,128)(2,1)}), bf16[8,64,768]{2,1,0:T(8,128)(2,1)}, u32[]{:S(2)}, u32[]{:S(2)}) %all-to-all-start) | async-done | bytes 786464 | tf_op jit(solution)/shard_map/all_to_all | solution.py:195
  318.7 18.7 %multiply_convert_fusion = (bf16[512,3072]{1,0:T(8,128)(2,1)}, f32[512,3072]{1,0:T(8,128)}, f32[512,3072]{1,0:T(8,128)}) fusion(bf16[512,768]{1,0:T(8,128)(2,1)} %bitcast.11, bf16[1,768,3072]{2,1,0:T(8,128)(2,1)} %all-gather.15.cloned.1.call-done), kind=kOutput, calls=%fused_computation.42 | convolution fusion | flops 2518155264 | bytes 21233664 | tf_op jit(solution)/shard_map/dot_general | solution.py:198
  349.5 10.2 %add_convert_fusion = bf16[512,3072]{1,0:T(8,128)(2,1)S(1)} fusion(f32[512,3072]{1,0:T(8,128)} %get-tuple-element.943, f32[512,3072]{1,0:T(8,128)} %get-tuple-element.958, bf16[512,768]{1,0:T(8,128)(2,1)} %bitcast.17, bf16[1,3072,768]{2,1,0:T(8,128)(2,1)} %all-gather.17.cloned.1.call-done), kind=kOutput, calls=%fused_computation.41 | convolution fusion | flops 2437939200 | bytes 21233664 | tf_op jit(solution)/shard_map/dot_general | solution.py:231
  377.4 18.4 %all-to-all-done.3 = bf16[8,64,768]{2,1,0:T(8,128)(2,1)} async-done(((bf16[8,64,768]{2,1,0:T(8,128)(2,1)}), bf16[8,64,768]{2,1,0:T(8,128)(2,1)}, u32[]{:S(2)}, u32[]{:S(2)}) %all-to-all-start.3) | async-done | bytes 786464 | tf_op jit(solution)/shard_map/all_to_all | solution.py:238
  412.5 295.4 %while.45 = (s32[]{:T(128)}, f32[256,12,64]{0,2,1:T(8,128)}, f32[1024,1536]{0,1:T(8,128)}, f32[12,2048]{1,0:T(8,128)}, bf16[1024,1536]{0,1:T(8,128)(2,1)S(1)}, /...) while((s32[]{:T(128)}, f32[256,12,64]{0,2,1:T(8,128)}, ...), condition=%wide.region_17.18_spmd.clone, body=%wide.region_15.17_spmd.clone.sunk | while | flops 1026621440 | bytes 326074112 | solution.py:50
  446.5 16.4 %copy.77 = f32[2,8,256,768]{3,1,2,0:T(8,128)} copy(f32[2,8,256,768]{3,2,1,0:T(8,128)} %bitcast.179) | data formatting | bytes 25165824 | tf_op jit(solution)/shard_map/while
  462.8 11.6 %slice.162 = f32[12,196352]{1,0:T(8,128)} slice(f32[12,196608]{1,0:T(8,128)} %bitcast.182), slice={[0:12], [255:196607]} | slice | bytes 18849792 | tf_op jit(solution)/shard_map/while/body/eval_jaxpr/slice | solution.py:109
  474.4 20.0 %reshape.366 = f32[12,256,767]{2,1,0:T(8,128)} reshape(f32[12,196352]{1,0:T(8,128)} %slice.162) | data formatting | bytes 18849792 | tf_op jit(solution)/shard_map/while/body/eval_jaxpr/reshape | solution.py:110
  526.6 13.1 %reshape.367 = bf16[12,196352]{1,0:T(8,128)(2,1)} reshape(bf16[12,256,767]{2,1,0:T(8,128)(2,1)} %pad.31.clone.2) | data formatting | bytes 9424896 | tf_op jit(solution)/shard_map/while/body/eval_jaxpr/reshape | solution.py:117
  549.7 12.8 %copy.80 = f32[2,8,256,768]{3,2,1,0:T(8,128)} copy(f32[2,8,256,768]{3,1,2,0:T(8,128)} %bitcast.180) | data formatting | bytes 25165824 | tf_op jit(solution)/shard_map/while
  578.2 16.4 %copy.77 = f32[2,8,256,768]{3,1,2,0:T(8,128)} copy(f32[2,8,256,768]{3,2,1,0:T(8,128)} %bitcast.179) | data formatting | bytes 25165824 | tf_op jit(solution)/shard_map/while
  594.6 11.6 %slice.162 = f32[12,196352]{1,0:T(8,128)} slice(f32[12,196608]{1,0:T(8,128)} %bitcast.182), slice={[0:12], [255:196607]} | slice | bytes 18849792 | tf_op jit(solution)/shard_map/while/body/eval_jaxpr/slice | solution.py:109
  606.2 20.0 %reshape.366 = f32[12,256,767]{2,1,0:T(8,128)} reshape(f32[12,196352]{1,0:T(8,128)} %slice.162) | data formatting | bytes 18849792 | tf_op jit(solution)/shard_map/while/body/eval_jaxpr/reshape | solution.py:110
  658.3 13.1 %reshape.367 = bf16[12,196352]{1,0:T(8,128)(2,1)} reshape(bf16[12,256,767]{2,1,0:T(8,128)(2,1)} %pad.31.clone.2) | data formatting | bytes 9424896 | tf_op jit(solution)/shard_map/while/body/eval_jaxpr/reshape | solution.py:117
  681.5 12.8 %copy.80 = f32[2,8,256,768]{3,2,1,0:T(8,128)} copy(f32[2,8,256,768]{3,1,2,0:T(8,128)} %bitcast.180) | data formatting | bytes 25165824 | tf_op jit(solution)/shard_map/while
  712.9 6.9 convolution_convert_fusion
  722.6 32.5 %reduce-scatter.5.cloned.1.call-done = bf16[256,1536]{0,1:T(8,128)(2,1)} async-done(((bf16[1024,1536]{0,1:T(8,128)(2,1)}), bf16[256,1536]{0,1:T(8,128)(2,1)}) %reduce-scatter.5.cloned.1.call-update) | async-done | bytes 786448 | tf_op jit(solution)/shard_map/reduce_scatter | solution.py:357
  760.7 7.2 convolution_convert_fusion.1
  772.6 40.9 %all-reduce.3 = (f32[768]{0:T(1024)}, f32[768]{0:T(1024)}, f32[32,12]{0,1:T(8,128)}, f32[768,8]{0,1:T(8,128)}) all-reduce(f32[768]{0:T(1024)S(1)} %get-tuple-element.888, f32[768]{0:T(1024)S(1)} %copy-done.50, f32[32,12]{0,1:T(8,128)S(1)} %fusion.44, f32[768,8]{0,1:T(8,128)S(1)} %fusion.58), channel_id=1, replica_groups=mesh['expert'=8,'shard'=4] {'expert','shard'}, use_global_device_ids=true, to_apply=%region_21.22 | all-reduce | flops 8064 | bytes 64512 | tf_op jit(solution)/shard_map/psum | solution.py:379
  819.4 57.2 %reduce-scatter.7.cloned.1.call-done = bf16[192,3072]{1,0:T(8,128)(2,1)} async-done(((bf16[768,3072]{1,0:T(8,128)(2,1)}), bf16[192,3072]{1,0:T(8,128)(2,1)}) %reduce-scatter.7.cloned.1.call-update) | async-done | bytes 1179664 | tf_op jit(solution)/shard_map/reduce_scatter | solution.py:368
  876.6 60.1 %reduce-scatter.9.cloned.1.call-done = bf16[192,3072]{1,0:T(8,128)(2,1)} async-done(((bf16[768,3072]{1,0:T(8,128)(2,1)}), bf16[192,3072]{1,0:T(8,128)(2,1)}) %reduce-scatter.9.cloned.1.call-update) | async-done | bytes 1179664 | tf_op jit(solution)/shard_map/reduce_scatter | solution.py:248
  939.7 58.9 %all-reduce.6.cloned.1.call-done = bf16[192,3072]{1,0:T(8,128)(2,1)} async-done(((bf16[192,3072]{1,0:T(8,128)(2,1)}), bf16[192,3072]{1,0:T(8,128)(2,1)}) %all-reduce.6.cloned.1.call-update) | async-done | bytes 1179664 | tf_op jit(solution)/shard_map/psum | solution.py:377
  (303 shorter events, 284.7 us)
Async XLA Ops:
  7.2 286.2 %copy-start = (f32[768,8]{0,1:T(8,128)S(1)}, f32[768,8]{0,1:T(8,128)}, u32[]{:S(2)}) copy-start(f32[768,8]{0,1:T(8,128)} %param.24) | copy-start | bytes 73732
  7.2 58.9 %copy-start.32 = (s32[256]{0:T(256)S(1)}, s32[256]{0:T(256)}, u32[]{:S(2)}) copy-start(s32[256]{0:T(256)} %param.18) | copy-start | bytes 3076
  7.2 66.9 %copy-start.36 = (s32[256,1]{0,1:T(1,128)S(1)}, s32[256,1]{0,1:T(1,128)}, u32[]{:S(2)}) copy-start(s32[256,1]{0,1:T(1,128)} %param.19) | copy-start | bytes 3076
  7.2 68.4 %copy-start.55 = (s32[2047]{0:T(1024)S(1)}, s32[2047]{0:T(1024)}, u32[]{:S(2)}) copy-start(s32[2047]{0:T(1024)} %param.20) | copy-start | bytes 24568
  7.2 68.4 %copy-start.54 = (f32[32,12]{0,1:T(8,128)S(1)}, f32[32,12]{0,1:T(8,128)}, u32[]{:S(2)}) copy-start(f32[32,12]{0,1:T(8,128)} %param.23) | copy-start | bytes 4612
  7.2 52.7 %all-gather.9.cloned.1.call-start = ((), (), s32[]{:S(2)}) async-start(), calls=%async_computation.8 | async-start | bytes 4423680 | tf_op jit(solution)/shard_map/all_gather | solution.py:79
  8.0 100.3 %all-gather.11.cloned.1.call-start = ((), (), s32[]{:S(2)}) async-start(), calls=%async_computation.9 | async-start | bytes 3932160 | tf_op jit(solution)/shard_map/all_gather | solution.py:167
  9.8 67.8 %copy-start.48 = (f32[256]{0:T(256)}, f32[256]{0:T(256)S(1)}, u32[]{:S(2)}) copy-start(f32[256]{0:T(256)S(1)} %get-tuple-element.953) | copy-start | bytes 3076
  64.1 220.3 %all-gather.13.cloned.1.call-start = ((), (), s32[]{:S(2)}) async-start(), calls=%async_computation.10 | async-start | bytes 1474560 | tf_op jit(solution)/shard_map/all_gather | solution.py:80
  64.9 253.9 %all-gather.15.cloned.1.call-start = ((), (), s32[]{:S(2)}) async-start(), calls=%async_computation.16 | async-start | bytes 5898240 | tf_op jit(solution)/shard_map/all_gather | solution.py:83
  65.5 272.0 %all-gather.17.cloned.1.call-start = ((), (), s32[]{:S(2)}) async-start(), calls=%async_computation.17 | async-start | bytes 5898240 | tf_op jit(solution)/shard_map/all_gather | solution.py:84
  111.5 175.9 %copy-start.34 = (f32[768]{0:T(1024)S(1)}, f32[768]{0:T(1024)}, u32[]{:S(2)}) copy-start(f32[768]{0:T(1024)} %param.22) | copy-start | bytes 9220
  111.5 175.9 %copy-start.43 = (s32[256]{0:T(256)S(1)}, s32[256]{0:T(256)}, u32[]{:S(2)}) copy-start(s32[256]{0:T(256)} %multiply_add_fusion) | copy-start | bytes 3076
  286.5 113.7 %copy-start.39 = (f32[256]{0:T(256)}, f32[256]{0:T(256)S(1)}, u32[]{:S(2)}) copy-start(f32[256]{0:T(256)S(1)} %get-tuple-element.955) | copy-start | bytes 3076
  288.7 25.8 %all-to-all-start = ((bf16[8,64,768]{2,1,0:T(8,128)(2,1)}), bf16[8,64,768]{2,1,0:T(8,128)(2,1)}, u32[]{:S(2)}, u32[]{:S(2)}) async-start(bf16[8,64,768]{2,1,0:T(8,128)(2,1)} %bitcast.197), calls=%async_computation | async-start | bytes 1572864 | tf_op jit(solution)/shard_map/all_to_all | solution.py:195
  295.4 102.0 %copy-start.30 = (f32[256,8]{0,1:T(8,128)}, f32[256,8]{0,1:T(8,128)S(1)}, u32[]{:S(2)}) copy-start(f32[256,8]{0,1:T(8,128)S(1)} %get-tuple-element.960) | copy-start | bytes 24580
  295.4 102.0 %copy-start.41 = (f32[256]{0:T(256)}, f32[256]{0:T(256)S(1)}, u32[]{:S(2)}) copy-start(f32[256]{0:T(256)S(1)} %get-tuple-element.959) | copy-start | bytes 3076
  295.5 102.0 %copy-start.46 = (f32[256]{0:T(256)}, f32[256]{0:T(256)S(1)}, u32[]{:S(2)}) copy-start(f32[256]{0:T(256)S(1)} %fusion.87) | copy-start | bytes 3076
  295.5 104.7 %copy-start.44 = (f32[256]{0:T(256)}, f32[256]{0:T(256)S(1)}, u32[]{:S(2)}) copy-start(f32[256]{0:T(256)S(1)} %select_reduce_fusion) | copy-start | bytes 3076
  314.5 29.8 %all-to-all-start.2 = ((bf16[8,64,768]{2,1,0:T(8,128)(2,1)}), bf16[8,64,768]{2,1,0:T(8,128)(2,1)}, u32[]{:S(2)}, u32[]{:S(2)}) async-start(bf16[8,64,768]{2,1,0:T(8,128)(2,1)} %bitcast.196), calls=%async_computation.2 | async-start | bytes 1572864 | tf_op jit(solution)/shard_map/all_to_all | solution.py:220
  344.3 26.3 %all-to-all-start.1 = ((bf16[8,64,768]{2,1,0:T(8,128)(2,1)}), bf16[8,64,768]{2,1,0:T(8,128)(2,1)}, u32[]{:S(2)}, u32[]{:S(2)}) async-start(bf16[8,64,768]{2,1,0:T(8,128)(2,1)} %bitcast.201), calls=%async_computation.1 | async-start | bytes 1572864 | tf_op jit(solution)/shard_map/all_to_all | solution.py:203
  370.5 25.2 %all-to-all-start.3 = ((bf16[8,64,768]{2,1,0:T(8,128)(2,1)}), bf16[8,64,768]{2,1,0:T(8,128)(2,1)}, u32[]{:S(2)}, u32[]{:S(2)}) async-start(bf16[8,64,768]{2,1,0:T(8,128)(2,1)} %bitcast.200), calls=%async_computation.3 | async-start | bytes 1572864 | tf_op jit(solution)/shard_map/all_to_all | solution.py:238
  374.8 380.4 %reduce-scatter.5.cloned.1.call-start = ((), (), s32[]{:S(2)}) async-start(), calls=%async_computation.11 | async-start | bytes 3932160 | tf_op jit(solution)/shard_map/reduce_scatter | solution.py:357
  440.0 67.2 %copy-start.3 = (bf16[512,768]{0,1:T(8,128)(2,1)}, bf16[512,768]{0,1:T(8,128)(2,1)S(1)}, u32[]{:S(2)}) copy-start(bf16[512,768]{0,1:T(8,128)(2,1)S(1)} %get-tuple-element.1119) | copy-start | bytes 2359300 | tf_op jit(solution)/shard_map/while
  571.8 67.2 %copy-start.3 = (bf16[512,768]{0,1:T(8,128)(2,1)}, bf16[512,768]{0,1:T(8,128)(2,1)S(1)}, u32[]{:S(2)}) copy-start(bf16[512,768]{0,1:T(8,128)(2,1)S(1)} %get-tuple-element.1119) | copy-start | bytes 2359300 | tf_op jit(solution)/shard_map/while
  712.8 103.7 %reduce-scatter.11.cloned.1.call-start = ((), (), s32[]{:S(2)}) async-start(), calls=%async_computation.15 | async-start | bytes 5898240 | tf_op jit(solution)/shard_map/reduce_scatter | solution.py:251
  719.8 35.3 %copy-start.49 = (f32[256]{0:T(256)S(1)}, f32[256]{0:T(256)}, u32[]{:S(2)}) copy-start(f32[256]{0:T(256)} %copy-done.48) | copy-start | bytes 3076
  719.9 156.7 %reduce-scatter.7.cloned.1.call-start = ((), (), s32[]{:S(2)}) async-start(), calls=%async_computation.12 | async-start | bytes 5898240 | tf_op jit(solution)/shard_map/reduce_scatter | solution.py:368
  760.6 176.1 %reduce-scatter.9.cloned.1.call-start = ((), (), s32[]{:S(2)}) async-start(), calls=%async_computation.14 | async-start | bytes 5898240 | tf_op jit(solution)/shard_map/reduce_scatter | solution.py:248
  767.9 45.7 %copy-start.53 = (f32[256]{0:T(256)S(1)}, f32[256]{0:T(256)}, u32[]{:S(2)}) copy-start(f32[256]{0:T(256)} %get-tuple-element.952) | copy-start | bytes 3076
  767.9 230.7 %all-reduce.6.cloned.1.call-start = ((), (), s32[]{:S(2)}) async-start(), calls=%async_computation.13 | async-start | bytes 2359296 | tf_op jit(solution)/shard_map/psum | solution.py:377
  813.6 189.3 %copy-start.1 = (f32[768,8]{0,1:T(8,128)S(1)}, f32[768,8]{0,1:T(8,128)}, u32[]{:S(2)}) copy-start(f32[768,8]{0,1:T(8,128)} %param.24) | copy-start | bytes 73732
  (58 other events, 374.5 us)
Sparse Core Ops, SparseCore 0:
  9.9 49.9 all-gather.8
  64.3 43.9 all-gather.10
  110.1 27.7 all-gather.12
  139.6 57.0 all-gather.14
  198.4 57.0 all-gather.16
  713.0 42.1 reduce-scatter.4
  758.1 58.3 reduce-scatter.10
  819.5 57.0 reduce-scatter.6
  879.6 57.0 reduce-scatter.8
  938.9 59.6 all-reduce.5
where the time goes:
time: 1020 us; the launch traced here: 1010 us
  local copies, waits for them, and re-layouts  372 us (36%)
  waiting for transfers between devices  332 us (33%)
  matrix products  118 us (12%)
  other arithmetic  56 us (5%)
  loops' own time  49.2 us (5%)
  blocking collectives  48.9 us (5%)
  starting transfers between devices  18.8 us (2%)
  between operations  15 us (1%)
    while x90, local copies, waits for them, and re-layouts  156 us
    reshape x4, local copies, waits for them, and re-layouts, bias_block(): return cut.reshape(heads, query_count, total - 1)[:, :, :key_count]  80.1 us
    reduce_scatter x1, waiting for transfers between devices, body(): lax.psum_scatter(grad_in_part.astype(jnp.bfloat16), 'shard', scatter_dime...  60.1 us
    psum x1, waiting for transfers between devices, body(): lax.psum(weight_rows.astype(jnp.bfloat16), 'expert').astype(jnp.float32)  58.9 us
    reduce_scatter x1, waiting for transfers between devices, body(): lax.psum_scatter(jnp.concatenate([contract_rows(normed_attn_b, grad_qkv_b...  57.2 us
    all_gather x1, waiting for transfers between devices, body(): lax.all_gather(qkv_weight, 'shard', axis=0, tiled=True)  50.1 us
    another operation x2, loops' own time, by_blocks(): return lax.fori_loop(0, total_rows // block_rows, advance, running)  49.2 us
    slice x4, local copies, waits for them, and re-layouts, bias_block(): cut = tiled[:, query_count - 1:query_count - 1 + query_count * (total - 1)]  46.3 us
  transfers between devices with their start and end apart: 14, of which 10 were waited for; matrix products, arithmetic and copies ran while one was open for 24% of the time, Pallas kernels for 0%

commit v1 on v0

v1 whole, which is shorter than its diff:
```python
from functools import partial

import jax
import jax.numpy as jnp
from jax import lax
from jax.experimental import pallas as pl
from jax.experimental.pallas import tpu as pltpu
from jax.sharding import PartitionSpec as P

epsilon = 1e-06
neg_large = -1000000000.0
highest = lax.Precision.HIGHEST
tile_rows = 128
vmem_grant = 40 * 1024 * 1024


def norm_rows(values, gain):
    inverse = lax.rsqrt(jnp.mean(values * values, axis=1, keepdims=True) + epsilon)
    return (values * inverse * gain, inverse)


def norm_back(values, inverse, gain, upstream):
    scaled = upstream * gain
    gain_grad = jnp.sum(upstream * values * inverse, axis=0)
    input_grad = inverse * scaled - values * inverse**3 * jnp.mean(
        scaled * values, axis=1, keepdims=True
    )
    return (input_grad, gain_grad)


def contract_rows(left, right, precision_level=None):
    return lax.dot_general(
        left,
        right,
        (((0,), (0,)), ((), ())),
        precision=precision_level,
        preferred_element_type=jnp.float32,
    )


def toeplitz_rows(seed, rows):
    grid = seed
    while grid.shape[0] < rows:
        grid = jnp.concatenate([grid, pltpu.roll(grid, grid.shape[0], 1)], axis=0)
    return grid


def fold_rows(grid):
    width = grid.shape[1]
    while grid.shape[0] > 8:
        half = grid.shape[0] // 2
        grid = grid[:half] + pltpu.roll(grid[half:], width - half, 1)
    return grid


def dot_last(left, right):
    return lax.dot_general(
        left, right, (((1,), (1,)), ((), ())), preferred_element_type=jnp.float32
    )


def attend_kernel(scale, q_ref, k_ref, v_ref, seed_ref, segq_ref, segk_ref, out_ref, log_ref):
    rows, lanes = q_ref.shape
    keys = k_ref.shape[0]
    left_half = lax.broadcasted_iota(jnp.int32, (tile_rows, lanes), 1) < lanes // 2
    key_part, value_part = k_ref[...], v_ref[...]
    seg_k = segk_ref[...]
    zero = jnp.zeros((), jnp.bfloat16)
    grids = [toeplitz_rows(seed_ref[head], tile_rows) for head in range(2)]
    for first in range(0, rows, tile_rows):
        here = pl.ds(first, tile_rows)
        allowed = segq_ref[here, :] == seg_k
        query = q_ref[here, :] * scale
        found = []
        for head in range(2):
            own = left_half if head == 0 else ~left_half
            start = rows - first
            scores = dot_last(jnp.where(own, query, zero), key_part)
            scores = scores + grids[head][:, start : start + keys]
            scores = jnp.where(allowed, scores, neg_large)
            top = jnp.max(scores, axis=1, keepdims=True)
            weights = jnp.exp(scores - top)
            total = jnp.sum(weights, axis=1, keepdims=True)
            mixed = jnp.dot(
                weights.astype(jnp.bfloat16), value_part, preferred_element_type=jnp.float32
            )
            found.append((mixed / total, top + jnp.log(total)))
        out_ref[here, :] = jnp.where(left_half, found[0][0], found[1][0])
        log_ref[here, :] = jnp.where(left_half, found[0][1], found[1][1])


def attend_back_kernel(
    scale,
    q_ref,
    k_ref,
    v_ref,
    seed_ref,
    segq_ref,
    segk_ref,
    att_ref,
    log_ref,
    grad_ref,
    dq_ref,
    dkv_ref,
    dbias_ref,
    weight_scr,
    score_scr,
    query_scr,
    grad_scr,
):
    rows, lanes = q_ref.shape
    keys = k_ref.shape[0]
    left_half = lax.broadcasted_iota(jnp.int32, (tile_rows, lanes), 1) < lanes // 2
    key_part, value_part = k_ref[...], v_ref[...]
    seg_k = segk_ref[...]
    zero = jnp.zeros((), jnp.bfloat16)
    grids = [toeplitz_rows(seed_ref[head], tile_rows) for head in range(2)]
    sums = [None, None]
    for first in range(0, rows, tile_rows):
        here = pl.ds(first, tile_rows)
        allowed = segq_ref[here, :] == seg_k
        query = q_ref[here, :] * scale
        grad = grad_ref[here, :]
        product = grad.astype(jnp.float32) * att_ref[here, :]
        log_rows = log_ref[here, :]
        found = []
        for head in range(2):
            own = left_half if head == 0 else ~left_half
            start = rows - first
            put = pl.ds(head * rows + first, tile_rows)
            query_own = jnp.where(own, query, zero)
            grad_own = jnp.where(own, grad, zero)
            query_scr[put, :] = query_own
            grad_scr[put, :] = grad_own
            delta = jnp.sum(jnp.where(own, product, 0.0), axis=1, keepdims=True)
            lane = head * (lanes // 2)
            scores = dot_last(query_own, key_part) + grids[head][:, start : start + keys]
            weights = jnp.where(
                allowed, jnp.exp(scores - log_rows[:, lane : lane + 1]), 0.0
            )
            weight_grad = dot_last(grad_own, value_part)
            score_grad = (weights * (weight_grad - delta)).astype(jnp.bfloat16)
            weight_scr[put, :] = weights.astype(jnp.bfloat16)
            score_scr[put, :] = score_grad
            found.append(jnp.dot(score_grad, key_part, preferred_element_type=jnp.float32))
            pieces = [jnp.zeros((tile_rows, start), jnp.float32), score_grad.astype(jnp.float32)]
            if first > 0:
                pieces.append(jnp.zeros((tile_rows, first), jnp.float32))
            placed = jnp.concatenate(pieces, axis=1)
            sums[head] = placed if sums[head] is None else sums[head] + placed
        dq_ref[here, :] = (jnp.where(left_half, found[0], found[1]) * scale).astype(jnp.bfloat16)
    for head in range(2):
        dbias_ref[head] = fold_rows(sums[head])
    dkv_ref[:, :lanes] = contract_rows(score_scr[...], query_scr[...]).astype(jnp.bfloat16)
    dkv_ref[:, lanes:] = contract_rows(weight_scr[...], grad_scr[...]).astype(jnp.bfloat16)


def pair_specs(rows, keys, pairs, lanes, window):
    return [
        pl.BlockSpec((rows, lanes), lambda i: (0, i)),
        pl.BlockSpec((keys, lanes), lambda i: (0, i)),
        pl.BlockSpec((keys, lanes), lambda i: (0, pairs + i)),
        pl.BlockSpec((2, 8, window), lambda i: (i, 0, 0)),
        pl.BlockSpec((rows, 1), lambda i: (0, 0)),
        pl.BlockSpec((1, keys), lambda i: (0, 0)),
    ]


def attend(qkv_b, kv_all, seeds, seg_q, seg_k, head_size):
    rows, keys = qkv_b.shape[0], kv_all.shape[0]
    width, lanes = kv_all.shape[1] // 2, 2 * head_size
    pairs, window = width // lanes, seeds.shape[2]
    here = pl.BlockSpec((rows, lanes), lambda i: (0, i))
    return pl.pallas_call(
        partial(attend_kernel, head_size ** (-0.5)),
        grid=(pairs,),
        in_specs=pair_specs(rows, keys, pairs, lanes, window),
        out_specs=[here, here],
        out_shape=[jax.ShapeDtypeStruct((rows, width), jnp.float32)] * 2,
        compiler_params=pltpu.CompilerParams(vmem_limit_bytes=vmem_grant),
        cost_estimate=pl.CostEstimate(
            flops=8 * rows * keys * width,
            bytes_accessed=4 * keys * width + 10 * rows * width,
            transcendentals=2 * pairs * rows * keys,
        ),
    )(qkv_b, kv_all, kv_all, seeds, seg_q, seg_k)


def attend_back(qkv_b, kv_all, seeds, seg_q, seg_k, attended32, log_rows, grad_attended, head_size):
    rows, keys = qkv_b.shape[0], kv_all.shape[0]
    width, lanes = kv_all.shape[1] // 2, 2 * head_size
    pairs, window = width // lanes, seeds.shape[2]
    here = pl.BlockSpec((rows, lanes), lambda i: (0, i))
    return pl.pallas_call(
        partial(attend_back_kernel, head_size ** (-0.5)),
        grid=(pairs,),
        in_specs=pair_specs(rows, keys, pairs, lanes, window) + [here, here, here],
        out_specs=[
            here,
            pl.BlockSpec((keys, 2 * lanes), lambda i: (0, i)),
            pl.BlockSpec((2, 8, window), lambda i: (i, 0, 0)),
        ],
        out_shape=[
            jax.ShapeDtypeStruct((rows, width), jnp.bfloat16),
            jax.ShapeDtypeStruct((keys, 2 * width), jnp.bfloat16),
            jax.ShapeDtypeStruct(seeds.shape, jnp.float32),
        ],
        scratch_shapes=[
            pltpu.VMEM((2 * rows, keys), jnp.bfloat16),
            pltpu.VMEM((2 * rows, keys), jnp.bfloat16),
            pltpu.VMEM((2 * rows, lanes), jnp.bfloat16),
            pltpu.VMEM((2 * rows, lanes), jnp.bfloat16),
        ],
        compiler_params=pltpu.CompilerParams(vmem_limit_bytes=vmem_grant),
        cost_estimate=pl.CostEstimate(
            flops=20 * rows * keys * width,
            bytes_accessed=8 * keys * width + 14 * rows * width,
            transcendentals=2 * pairs * rows * keys,
        ),
    )(qkv_b, kv_all, kv_all, seeds, seg_q, seg_k, attended32, log_rows, grad_attended)


def body(
    tokens,
    segments,
    routes,
    buckets,
    gain_attn,
    gain_moe,
    rel_table,
    router_weight,
    qkv_weight,
    out_weight,
    w_in,
    w_out,
    out_grad,
):
    rows_here = tokens.shape[0]
    width = tokens.shape[1]
    heads = rel_table.shape[1]
    head_size = width // heads
    experts = router_weight.shape[1]
    capacity = 2 * rows_here // experts
    score_scale = head_size ** (-0.5)
    shard_count = lax.axis_size("shard")
    query_base = lax.axis_index("shard") * rows_here
    qkv_full, out_full = (
        lax.all_gather(qkv_weight, "shard", axis=0, tiled=True),
        lax.all_gather(out_weight, "shard", axis=0, tiled=True),
    )
    in_full, out_ff_full = (
        lax.all_gather(w_in[0], "shard", axis=0, tiled=True),
        lax.all_gather(w_out[0], "shard", axis=0, tiled=True),
    )
    inputs32 = tokens.astype(jnp.float32)
    normed_attn, inverse_attn = norm_rows(inputs32, gain_attn)
    normed_attn_b = normed_attn.astype(jnp.bfloat16)
    qkv_b = jnp.dot(normed_attn_b, qkv_full, preferred_element_type=jnp.float32).astype(
        jnp.bfloat16
    )
    key_value = qkv_b[:, width:]
    bucket_onehot = jax.nn.one_hot(buckets, rel_table.shape[0], dtype=jnp.float32)
    offsets_t = jnp.dot(
        bucket_onehot, rel_table, precision=highest, preferred_element_type=jnp.float32
    ).T
    length = shard_count * rows_here
    window = length + rows_here
    window_first = length - rows_here - query_base
    offsets_pad = jnp.concatenate([jnp.zeros((heads, 1), jnp.float32), offsets_t], axis=1)
    offsets_here = lax.dynamic_slice_in_dim(offsets_pad, window_first, window, 1)
    seeds = jnp.stack([jnp.roll(offsets_here, row, axis=1) for row in range(8)], axis=1)
    kv_all = lax.all_gather(key_value, "shard", axis=0, tiled=True)
    seg_k = lax.all_gather(segments, "shard", axis=0, tiled=True)[None, :]
    seg_q = segments[:, None]
    attended32, log_rows = attend(qkv_b, kv_all, seeds, seg_q, seg_k, head_size)
    attended_b = attended32.astype(jnp.bfloat16)
    hidden1 = inputs32 + jnp.dot(attended_b, out_full, preferred_element_type=jnp.float32)
    normed_moe, inverse_moe = norm_rows(hidden1, gain_moe)
    logits = jnp.dot(
        normed_moe, router_weight, precision=highest, preferred_element_type=jnp.float32
    )
    router_probs = jax.nn.softmax(logits, axis=1)
    route = routes[:, 0]
    route_onehot = (route[:, None] == jnp.arange(experts, dtype=jnp.int32)[None, :]).astype(
        jnp.float32
    )
    gate = jnp.sum(router_probs * route_onehot, axis=1)
    onehot_count = route_onehot.astype(jnp.int32)
    rank_in_expert = jnp.sum((jnp.cumsum(onehot_count, axis=0) - 1) * onehot_count, axis=1)
    slot_id = route * capacity + rank_in_expert
    dispatch = (
        jnp.arange(experts * capacity, dtype=jnp.int32)[:, None] == slot_id[None, :]
    ).astype(jnp.bfloat16)
    send_rows = jnp.dot(
        dispatch, normed_moe.astype(jnp.bfloat16), preferred_element_type=jnp.float32
    ).astype(jnp.bfloat16)
    send_rows = send_rows.reshape(experts, capacity, width)
    received = lax.all_to_all(send_rows, "expert", split_axis=0, concat_axis=0, tiled=True)
    sources = received.shape[0]
    item_count = received.shape[1]
    pre = jnp.dot(received.reshape(-1, width), in_full, preferred_element_type=jnp.float32)
    hidden_ff = jax.nn.gelu(pre, approximate=False).astype(jnp.bfloat16)
    result = jnp.dot(hidden_ff, out_ff_full, preferred_element_type=jnp.float32).astype(
        jnp.bfloat16
    )
    returned_rows = lax.all_to_all(
        result.reshape(sources, item_count, width),
        "expert",
        split_axis=0,
        concat_axis=0,
        tiled=True,
    )
    pre_kept = pre.reshape(sources, item_count, -1)
    expert_out = contract_rows(dispatch, returned_rows.reshape(-1, width))
    output = (hidden1 + gate[:, None] * expert_out).astype(jnp.bfloat16)
    upstream = out_grad.astype(jnp.float32)
    gate_grad = jnp.sum(upstream * expert_out, axis=1)
    grad_slots = jnp.dot(
        dispatch,
        (gate[:, None] * upstream).astype(jnp.bfloat16),
        preferred_element_type=jnp.float32,
    ).astype(jnp.bfloat16)
    grad_received = lax.all_to_all(
        grad_slots.reshape(experts, capacity, width),
        "expert",
        split_axis=0,
        concat_axis=0,
        tiled=True,
    )
    grad_flat = grad_received.reshape(-1, width)
    pre_flat = pre_kept.reshape(grad_flat.shape[0], -1)
    hidden_ff, gelu_back = jax.vjp(partial(jax.nn.gelu, approximate=False), pre_flat)
    hidden_b = hidden_ff.astype(jnp.bfloat16)
    grad_hidden = lax.dot_general(
        grad_flat, out_ff_full, (((1,), (1,)), ((), ())), preferred_element_type=jnp.float32
    )
    grad_pre = gelu_back(grad_hidden)[0].astype(jnp.bfloat16)
    grad_back_rows = lax.dot_general(
        grad_pre, in_full, (((1,), (1,)), ((), ())), preferred_element_type=jnp.float32
    ).astype(jnp.bfloat16)
    returned_grad = lax.all_to_all(
        grad_back_rows.reshape(grad_received.shape),
        "expert",
        split_axis=0,
        concat_axis=0,
        tiled=True,
    )
    grad_in_part = contract_rows(received.reshape(-1, width), grad_pre)
    grad_out_part = contract_rows(hidden_b, grad_flat)
    grad_in_rows, grad_out_rows = (
        lax.psum_scatter(
            grad_in_part.astype(jnp.bfloat16), "shard", scatter_dimension=0, tiled=True
        ).astype(jnp.float32),
        lax.psum_scatter(
            grad_out_part.astype(jnp.bfloat16), "shard", scatter_dimension=0, tiled=True
        ).astype(jnp.float32),
    )
    grad_expert_in = contract_rows(dispatch, returned_grad.reshape(-1, width))
    logit_grad = gate_grad[:, None] * router_probs * (route_onehot - gate[:, None])
    router_grad = contract_rows(normed_moe, logit_grad, highest)
    grad_normed_moe = grad_expert_in + lax.dot_general(
        logit_grad,
        router_weight,
        (((1,), (1,)), ((), ())),
        precision=highest,
        preferred_element_type=jnp.float32,
    )
    grad_moe_in, gain_moe_grad = norm_back(hidden1, inverse_moe, gain_moe, grad_normed_moe)
    grad_hidden1 = upstream + grad_moe_in
    branch_grad = grad_hidden1.astype(jnp.bfloat16)
    grad_attended = lax.dot_general(
        branch_grad, out_full, (((1,), (1,)), ((), ())), preferred_element_type=jnp.float32
    ).astype(jnp.bfloat16)
    query_grad, pair_grads, seed_grads = attend_back(
        qkv_b, kv_all, seeds, seg_q, seg_k, attended32, log_rows, grad_attended, head_size
    )
    kv_grad = lax.psum_scatter(pair_grads, "shard", scatter_dimension=0, tiled=True)
    kv_grad = kv_grad.reshape(rows_here, heads // 2, 2, 2 * head_size)
    kv_grad = kv_grad.transpose(0, 2, 1, 3).reshape(rows_here, 2 * width)
    grad_qkv_b = jnp.concatenate([query_grad, kv_grad], axis=1)
    grad_normed_attn = lax.dot_general(
        grad_qkv_b, qkv_full, (((1,), (1,)), ((), ())), preferred_element_type=jnp.float32
    )
    grad_attn_in, gain_attn_grad = norm_back(inputs32, inverse_attn, gain_attn, grad_normed_attn)
    grad_tokens = grad_hidden1 + grad_attn_in
    weight_rows = lax.psum_scatter(
        jnp.concatenate(
            [contract_rows(normed_attn_b, grad_qkv_b), contract_rows(attended_b, branch_grad)],
            axis=1,
        ).astype(jnp.bfloat16),
        "shard",
        scatter_dimension=0,
        tiled=True,
    ).astype(jnp.float32)
    weight_rows = lax.psum(weight_rows.astype(jnp.bfloat16), "expert").astype(jnp.float32)
    window_grad = sum(jnp.roll(seed_grads[:, row], -row, axis=1) for row in range(8))
    onehot_pad = jnp.concatenate([jnp.zeros_like(bucket_onehot[:1]), bucket_onehot], axis=0)
    onehot_here = lax.dynamic_slice_in_dim(onehot_pad, window_first, window, 0)
    table_grad = jnp.dot(
        window_grad, onehot_here, precision=highest, preferred_element_type=jnp.float32
    ).T
    gain_attn_total, gain_moe_total, table_total, router_total = lax.psum(
        (gain_attn_grad, gain_moe_grad, table_grad, router_grad), ("expert", "shard")
    )
    return (
        output,
        grad_tokens,
        gain_attn_total,
        gain_moe_total,
        table_total,
        router_total,
        weight_rows[:, : 3 * width],
        weight_rows[:, 3 * width :],
        grad_in_rows[None],
        grad_out_rows[None],
    )


def solution(mesh):
    in_specs = (
        P(("expert", "shard"), None),
        P(("expert", "shard")),
        P(("expert", "shard"), None),
        P(),
        P(),
        P(),
        P(),
        P(),
        P("shard", None),
        P("shard", None),
        P("expert", "shard", None),
        P("expert", "shard", None),
        P(("expert", "shard"), None),
    )
    out_specs = (
        P(("expert", "shard"), None),
        P(("expert", "shard"), None),
        P(),
        P(),
        P(),
        P(),
        P("shard", None),
        P("shard", None),
        P("expert", "shard", None),
        P("expert", "shard", None),
    )
    return jax.shard_map(body, mesh=mesh, in_specs=in_specs, out_specs=out_specs, check_vma=False)
```

time: 1020 us -> 651 us (0.64)
  local copies, waits for them, and re-layouts: 372 us -> 21.4 us
  waiting for transfers between devices: 332 us -> 418 us
  loops' own time: 49.2 us -> 0 us
  other arithmetic: 56 us -> 15 us
  matrix products: 118 us -> 79.4 us
  Pallas kernels: 0 us -> 27 us
    while x90 -> x0, local copies, waits for them, and re-layouts: 156 us -> none
    reshape x6 -> x2, local copies, waits for them, and re-layouts: 106 us -> 4.15 us  [body(): kv_grad = kv_grad.reshape(rows_here, heads // 2, 2, 2 * head_size)]
    slice x14 -> x29, local copies, waits for them, and re-layouts: 79 us -> 1.86 us  [the longest x14 1.24 us: body(): jnp.roll(offsets_here, row, axis=1)]
    another operation x2 -> x0, loops' own time: 49.2 us -> none  [by_blocks(): return lax.fori_loop(0, total_rows // block_rows, advance, running)]
    all_gather x1, waiting for transfers between devices: 0.01 us -> 40.2 us  [body(): lax.all_gather(w_out[0], 'shard', axis=0, tiled=True)]
    dot_general x14 -> x1, matrix products: 33.2 us -> 0.48 us  [body(): jnp.dot(window_grad, onehot_here, precision=highest, preferred_element_ty...]
    pallas_call x0 -> x2, Pallas kernels: none -> 27 us  [the longest x1 15.5 us: attend_back(): pl.pallas_call(partial(attend_back_kernel, head_size ** (-0.5)), grid=(pa...]
    all_gather x1, waiting for transfers between devices: 0.02 us -> 25.5 us  [body(): lax.all_gather(w_in[0], 'shard', axis=0, tiled=True)]
  transfers between devices with their start and end apart: 14 -> 14, of which waited for: 10 -> 12; matrix products, arithmetic and copies ran while one was open for 24% -> 12% of each run, Pallas kernels for 0% -> 2%
where the time goes in v1:
time: 651 us; the launch traced here: 644 us
  waiting for transfers between devices  418 us (64%)
  matrix products  79.4 us (12%)
  blocking collectives  49.2 us (8%)
  Pallas kernels  27 us (4%)
  local copies, waits for them, and re-layouts  21.4 us (3%)
  starting transfers between devices  18.7 us (3%)
  between operations  15.4 us (2%)
  other arithmetic  15 us (2%)
    reduce_scatter x1, waiting for transfers between devices, body(): lax.psum_scatter(grad_in_part.astype(jnp.bfloat16), 'shard', scatter_dime...  60.1 us
    psum x1, waiting for transfers between devices, body(): lax.psum(weight_rows.astype(jnp.bfloat16), 'expert').astype(jnp.float32)  58.9 us
    reduce_scatter x1, waiting for transfers between devices, body(): lax.psum_scatter(jnp.concatenate([contract_rows(normed_attn_b, grad_qkv_b...  53.6 us
    all_gather x1, waiting for transfers between devices, body(): lax.all_gather(qkv_weight, 'shard', axis=0, tiled=True)  50.7 us
    psum x1, blocking collectives, body(): lax.psum((gain_attn_grad, gain_moe_grad, table_grad, router_grad), ('expe...  41.2 us
    all_gather x1, waiting for transfers between devices, body(): lax.all_gather(w_out[0], 'shard', axis=0, tiled=True)  40.2 us
    reduce_scatter x1, waiting for transfers between devices, body(): lax.psum_scatter(pair_grads, 'shard', scatter_dimension=0, tiled=True)  32.4 us
    all_gather x1, waiting for transfers between devices, body(): kv_all = lax.all_gather(key_value, 'shard', axis=0, tiled=True)  28.9 us
  transfers between devices with their start and end apart: 14, of which 12 were waited for; matrix products, arithmetic and copies ran while one was open for 12% of the time, Pallas kernels for 2%

profile of v1, /device:TPU:0, one launch (start us, length us, event | category | flops | bytes accessed | tf_op | source)
XLA Modules:
  0.0 644.3 jit_solution(53075046345668134)
XLA Ops:
  9.2 50.7 %all-gather.9.cloned.1.call-done = bf16[768,2304]{1,0:T(8,128)(2,1)} async-done(((bf16[192,2304]{1,0:T(8,128)(2,1)}), bf16[768,2304]{1,0:T(8,128)(2,1)}) %all-gather.9.cloned.1.call-update) | async-done | bytes 3538960 | tf_op jit(solution)/shard_map/all_gather | solution.py:248
  59.9 3.3 convolution_convert_fusion.3.q_ref
  71.4 8.0 %all-gather.2 = s32[4,1,256]{2,1,0:T(1,128)S(1)} all-gather(s32[1,1,256]{2,1,0:T(1,128)S(1)} %bitcast.124), channel_id=1, replica_groups=mesh['expert'=8,'shard'=4] {'shard'}, dimensions={0}, use_global_device_ids=true | all-gather | bytes 5120 | tf_op jit(solution)/shard_map/all_gather | solution.py:273
  79.5 28.9 %all-gather.11.cloned.1.call-done.k_ref.v_ref = bf16[1024,1536]{1,0:T(8,128)(2,1)} async-done(((bf16[256,1536]{1,0:T(8,128)(2,1)}), bf16[1024,1536]{1,0:T(8,128)(2,1)}) %all-gather.11.cloned.1.call-update) | async-done | bytes 3145744 | tf_op jit(solution)/shard_map/all_gather | solution.py:272
  110.3 11.5 %shard_map.204 = (f32[256,768]{1,0:T(8,128)S(1)}, f32[256,768]{1,0:T(8,128)S(1)}) custom-call(bf16[256,2304]{1,0:T(8,128)(2,1)S(1)} %convolution_convert_fusion.3.q_ref, bf16[1024,1536]{1,0:T(8,128)(2,1)S(1)} %copy-done.1, bf16[1024,1536]{1,0:T(8,128)(2,1)S(1)} %copy-done.1, f32[12,8,1280]{2,1,0:T(8,128)S(1)} %stack.35.seed_ref, ...), custom_call_target="tpu_custom_call" | custom-call | flops 1610612736 | bytes 5111808 | tf_op jit(solution)/shard_map/pallas_call | solution.py:174
  122.7 15.3 %all-gather.13.cloned.1.call-done = bf16[768,768]{1,0:T(8,128)(2,1)} async-done(((bf16[192,768]{1,0:T(8,128)(2,1)}), bf16[768,768]{1,0:T(8,128)(2,1)}) %all-gather.13.cloned.1.call-update) | async-done | bytes 1179664 | tf_op jit(solution)/shard_map/all_gather | solution.py:249
  141.3 4.6 all-to-all-start
  149.2 17.7 %all-to-all-done = bf16[8,64,768]{2,1,0:T(8,128)(2,1)S(1)} async-done(((bf16[8,64,768]{2,1,0:T(8,128)(2,1)}), bf16[8,64,768]{2,1,0:T(8,128)(2,1)S(1)}, u32[]{:S(2)}, u32[]{:S(2)}) %all-to-all-start) | async-done | bytes 786464 | tf_op jit(solution)/shard_map/all_to_all | solution.py:298
  166.9 4.4 all-to-all-start.2
  171.3 25.5 %all-gather.15.cloned.1.call-done = bf16[1,768,3072]{2,1,0:T(8,128)(2,1)} async-done(((bf16[1,192,3072]{2,1,0:T(8,128)(2,1)}), bf16[1,768,3072]{2,1,0:T(8,128)(2,1)}) %all-gather.15.cloned.1.call-update) | async-done | bytes 4718608 | tf_op jit(solution)/shard_map/all_gather | solution.py:252
  196.8 18.6 %multiply_convert_fusion = (bf16[512,3072]{1,0:T(8,128)(2,1)}, f32[512,3072]{1,0:T(8,128)}, f32[512,3072]{1,0:T(8,128)}) fusion(bf16[512,768]{1,0:T(8,128)(2,1)S(1)} %bitcast.113, bf16[1,768,3072]{2,1,0:T(8,128)(2,1)} %all-gather.15.cloned.1.call-done), kind=kOutput, calls=%fused_computation.3 | convolution fusion | flops 2518155264 | bytes 21233664 | tf_op jit(solution)/shard_map/dot_general | solution.py:301
  215.4 40.2 %all-gather.17.cloned.1.call-done = bf16[1,3072,768]{2,1,0:T(8,128)(2,1)} async-done(((bf16[1,768,768]{2,1,0:T(8,128)(2,1)}), bf16[1,3072,768]{2,1,0:T(8,128)(2,1)}) %all-gather.17.cloned.1.call-update) | async-done | bytes 4718608 | tf_op jit(solution)/shard_map/all_gather | solution.py:253
  255.6 10.4 %add_convert_fusion = bf16[512,3072]{1,0:T(8,128)(2,1)S(1)} fusion(f32[512,3072]{1,0:T(8,128)} %get-tuple-element.29, f32[512,3072]{1,0:T(8,128)} %get-tuple-element.44, bf16[512,768]{1,0:T(8,128)(2,1)} %bitcast.21, bf16[1,3072,768]{2,1,0:T(8,128)(2,1)} %all-gather.17.cloned.1.call-done), kind=kOutput, calls=%fused_computation.2 | convolution fusion | flops 2437939200 | bytes 21233664 | tf_op jit(solution)/shard_map/dot_general | solution.py:334
  266.0 3.5 fusion.16
  269.6 4.6 all-to-all-start.3
  274.2 6.8 %fusion.19 = bf16[512,768]{1,0:T(8,128)(2,1)} fusion(bf16[512,3072]{1,0:T(8,128)(2,1)} %get-tuple-element.28, bf16[1,3072,768]{2,1,0:T(8,128)(2,1)} %all-gather.17.cloned.1.call-done), kind=kOutput, calls=%fused_computation.39 | convolution fusion | flops 2416312320 | bytes 8650752 | tf_op jit(solution)/shard_map/dot_general | solution.py:303
  280.9 14.2 %all-to-all-done.3 = bf16[8,64,768]{2,1,0:T(8,128)(2,1)S(1)} async-done(((bf16[8,64,768]{2,1,0:T(8,128)(2,1)}), bf16[8,64,768]{2,1,0:T(8,128)(2,1)S(1)}, u32[]{:S(2)}, u32[]{:S(2)}) %all-to-all-start.3) | async-done | bytes 786464 | tf_op jit(solution)/shard_map/all_to_all | solution.py:341
  296.0 4.2 all-to-all-start.1
  300.5 2.6 fusion.38
  303.1 18.1 %all-to-all-done.1 = bf16[8,64,768]{2,1,0:T(8,128)(2,1)} async-done(((bf16[8,64,768]{2,1,0:T(8,128)(2,1)}), bf16[8,64,768]{2,1,0:T(8,128)(2,1)}, u32[]{:S(2)}, u32[]{:S(2)}) %all-to-all-start.1) | async-done | bytes 786464 | tf_op jit(solution)/shard_map/all_to_all | solution.py:306
  328.8 15.5 %shard_map.205 = (bf16[256,768]{1,0:T(8,128)(2,1)S(1)}, bf16[1024,1536]{1,0:T(8,128)(2,1)S(1)}, f32[12,8,1280]{2,1,0:T(8,128)S(1)}) custom-call(bf16[256,2304]{1,0:T(8,128)(2,1)S(1)} %copy-done.4, bf16[1024,1536]{1,0:T(8,128)(2,1)S(1)} %copy-done.2, bf16[1024,1536]{1,0:T(8,128)(2,1)S(1)} %copy-done.2, f32[12,8,1280]{2,1,0:T(8,128)S(1)} %copy-done.10, ...), custom_call_target="tpu_custom_call" | custom-call | flops 4026531840 | bytes 9043968 | tf_op jit(solution)/shard_map/pallas_call | solution.py:194
  347.6 7.0 %convolution_convert_fusion = bf16[3072,768]{1,0:T(8,128)(2,1)} fusion(bf16[512,3072]{1,0:T(8,128)(2,1)} %get-tuple-element.28, bf16[512,768]{1,0:T(8,128)(2,1)} %bitcast.21), kind=kOutput, calls=%fused_computation.17 | convolution fusion | flops 2418278400 | bytes 8650752 | tf_op jit(solution)/shard_map/dot_general | solution.py:32
  357.1 32.4 %reduce-scatter.5.cloned.1.call-done = bf16[256,1536]{1,0:T(8,128)(2,1)} async-done(((bf16[1024,1536]{1,0:T(8,128)(2,1)}), bf16[256,1536]{1,0:T(8,128)(2,1)}) %reduce-scatter.5.cloned.1.call-update) | async-done | bytes 786448 | tf_op jit(solution)/shard_map/reduce_scatter | solution.py:377
  396.2 2.8 pad_maximum_fusion
  399.4 6.3 convolution_convert_fusion.1
  408.2 3.7 fusion.32
  411.9 41.2 %all-reduce.2 = (f32[768]{0:T(1024)}, f32[768]{0:T(1024)}, f32[32,12]{0,1:T(8,128)}, f32[768,8]{0,1:T(8,128)}) all-reduce(f32[768]{0:T(1024)S(1)} %get-tuple-element.22, f32[768]{0:T(1024)S(1)} %get-tuple-element.20, f32[32,12]{0,1:T(8,128)S(1)} %fusion.34, ...), channel_id=1, replica_groups=mesh['expert'=8,'shard'=4] {'expert','shard'}, use_global_device_ids=true, to_apply=%region_13.14 | all-reduce | flops 8064 | bytes 64512 | tf_op jit(solution)/shard_map/psum | solution.py:402
  454.2 2.8 bitcast_convert_fusion
  457.1 53.6 %reduce-scatter.7.cloned.1.call-done = bf16[192,3072]{1,0:T(8,128)(2,1)} async-done(((bf16[768,3072]{1,0:T(8,128)(2,1)}), bf16[192,3072]{1,0:T(8,128)(2,1)}) %reduce-scatter.7.cloned.1.call-update) | async-done | bytes 1179664 | tf_op jit(solution)/shard_map/reduce_scatter | solution.py:386
  510.8 60.1 %reduce-scatter.9.cloned.1.call-done = bf16[192,3072]{1,0:T(8,128)(2,1)} async-done(((bf16[768,3072]{1,0:T(8,128)(2,1)}), bf16[192,3072]{1,0:T(8,128)(2,1)}) %reduce-scatter.9.cloned.1.call-update) | async-done | bytes 1179664 | tf_op jit(solution)/shard_map/reduce_scatter | solution.py:351
  570.9 2.9 bitcast_convert_fusion.1
  573.8 58.9 %all-reduce.5.cloned.1.call-done = bf16[192,3072]{1,0:T(8,128)(2,1)} async-done(((bf16[192,3072]{1,0:T(8,128)(2,1)}), bf16[192,3072]{1,0:T(8,128)(2,1)}) %all-reduce.5.cloned.1.call-update) | async-done | bytes 1179664 | tf_op jit(solution)/shard_map/psum | solution.py:395
  (181 shorter events, 48.4 us)
Async XLA Ops:
  7.2 138.7 %copy-start = (f32[768,8]{0,1:T(8,128)S(1)}, f32[768,8]{0,1:T(8,128)}, u32[]{:S(2)}) copy-start(f32[768,8]{0,1:T(8,128)} %param.20) | copy-start | bytes 73732
  7.2 58.9 %copy-start.35 = (f32[32,12]{0,1:T(8,128)S(1)}, f32[32,12]{0,1:T(8,128)}, u32[]{:S(2)}) copy-start(f32[32,12]{0,1:T(8,128)} %param.19) | copy-start | bytes 4612
  7.2 58.9 %copy-start.32 = (s32[2047]{0:T(1024)S(1)}, s32[2047]{0:T(1024)}, u32[]{:S(2)}) copy-start(s32[2047]{0:T(1024)} %param.16) | copy-start | bytes 24568
  7.2 52.7 %all-gather.9.cloned.1.call-start = ((), (), s32[]{:S(2)}) async-start(), calls=%async_computation.8 | async-start | bytes 4423680 | tf_op jit(solution)/shard_map/all_gather | solution.py:248
  7.9 100.5 %all-gather.11.cloned.1.call-start = ((), (), s32[]{:S(2)}) async-start(), calls=%async_computation.9 | async-start | bytes 3932160 | tf_op jit(solution)/shard_map/all_gather | solution.py:272
  63.2 58.7 %copy-start.3 = (bf16[256,2304]{1,0:T(8,128)(2,1)}, bf16[256,2304]{1,0:T(8,128)(2,1)S(1)}, u32[]{:S(2)}) copy-start(bf16[256,2304]{1,0:T(8,128)(2,1)S(1)} %convolution_convert_fusion.3.q_ref) | copy-start | bytes 3538948
  64.2 73.9 %all-gather.13.cloned.1.call-start = ((), (), s32[]{:S(2)}) async-start(), calls=%async_computation.10 | async-start | bytes 1474560 | tf_op jit(solution)/shard_map/all_gather | solution.py:249
  64.9 132.0 %all-gather.15.cloned.1.call-start = ((), (), s32[]{:S(2)}) async-start(), calls=%async_computation.16 | async-start | bytes 5898240 | tf_op jit(solution)/shard_map/all_gather | solution.py:252
  65.5 190.2 %all-gather.17.cloned.1.call-start = ((), (), s32[]{:S(2)}) async-start(), calls=%async_computation.17 | async-start | bytes 5898240 | tf_op jit(solution)/shard_map/all_gather | solution.py:253
  67.8 70.3 %copy-start.21 = (bf16[256,768]{1,0:T(8,128)(2,1)S(1)}, bf16[256,768]{1,0:T(8,128)(2,1)}, u32[]{:S(2)}) copy-start(bf16[256,768]{1,0:T(8,128)(2,1)} %param.13) | copy-start | bytes 1179652
  69.5 70.4 %copy-start.30 = (f32[768]{0:T(1024)S(1)}, f32[768]{0:T(1024)}, u32[]{:S(2)}) copy-start(f32[768]{0:T(1024)} %param.18) | copy-start | bytes 9220
  71.4 69.9 %copy-start.9 = (f32[12,8,1280]{2,1,0:T(8,128)}, f32[12,8,1280]{2,1,0:T(8,128)S(1)}, u32[]{:S(2)}) copy-start(f32[12,8,1280]{2,1,0:T(8,128)S(1)} %stack.35.seed_ref) | copy-start | bytes 1474564
  122.7 92.7 %copy-start.6 = (f32[256,768]{1,0:T(8,128)}, f32[256,768]{1,0:T(8,128)S(1)}, u32[]{:S(2)}) copy-start(f32[256,768]{1,0:T(8,128)S(1)} %get-tuple-element.15.att_ref) | copy-start | bytes 2359300
  139.9 75.5 %copy-start.17 = (f32[256,768]{1,0:T(8,128)}, f32[256,768]{1,0:T(8,128)S(1)}, u32[]{:S(2)}) copy-start(f32[256,768]{1,0:T(8,128)S(1)} %get-tuple-element.43) | copy-start | bytes 2359300
  141.3 25.6 %all-to-all-start = ((bf16[8,64,768]{2,1,0:T(8,128)(2,1)}), bf16[8,64,768]{2,1,0:T(8,128)(2,1)S(1)}, u32[]{:S(2)}, u32[]{:S(2)}) async-start(bf16[8,64,768]{2,1,0:T(8,128)(2,1)} %bitcast.109), calls=%async_computation | async-start | bytes 1572864 | tf_op jit(solution)/shard_map/all_to_all | solution.py:298
  166.9 48.6 %copy-start.27 = (bf16[8,64,768]{2,1,0:T(8,128)(2,1)}, bf16[8,64,768]{2,1,0:T(8,128)(2,1)S(1)}, u32[]{:S(2)}) copy-start(bf16[8,64,768]{2,1,0:T(8,128)(2,1)S(1)} %all-to-all-done) | copy-start | bytes 2359300
  166.9 88.8 %all-to-all-start.2 = ((bf16[8,64,768]{2,1,0:T(8,128)(2,1)}), bf16[8,64,768]{2,1,0:T(8,128)(2,1)}, u32[]{:S(2)}, u32[]{:S(2)}) async-start(bf16[8,64,768]{2,1,0:T(8,128)(2,1)} %bitcast.20), calls=%async_computation.2 | async-start | bytes 1572864 | tf_op jit(solution)/shard_map/all_to_all | solution.py:323
  255.6 10.4 %copy-start.34 = (bf16[1,768,3072]{2,1,0:T(8,128)(2,1)S(1)}, bf16[1,768,3072]{2,1,0:T(8,128)(2,1)}, u32[]{:S(2)}) copy-start(bf16[1,768,3072]{2,1,0:T(8,128)(2,1)} %all-gather.15.cloned.1.call-done) | copy-start | bytes 14155780
  269.6 25.6 %all-to-all-start.3 = ((bf16[8,64,768]{2,1,0:T(8,128)(2,1)}), bf16[8,64,768]{2,1,0:T(8,128)(2,1)S(1)}, u32[]{:S(2)}, u32[]{:S(2)}) async-start(bf16[8,64,768]{2,1,0:T(8,128)(2,1)} %bitcast.22), calls=%async_computation.3 | async-start | bytes 1572864 | tf_op jit(solution)/shard_map/all_to_all | solution.py:341
  296.0 25.2 %all-to-all-start.1 = ((bf16[8,64,768]{2,1,0:T(8,128)(2,1)}), bf16[8,64,768]{2,1,0:T(8,128)(2,1)}, u32[]{:S(2)}, u32[]{:S(2)}) async-start(bf16[8,64,768]{2,1,0:T(8,128)(2,1)} %bitcast.18), calls=%async_computation.1 | async-start | bytes 1572864 | tf_op jit(solution)/shard_map/all_to_all | solution.py:306
  300.3 28.5 %copy-start.2 = (bf16[1024,1536]{1,0:T(8,128)(2,1)S(1)}, bf16[1024,1536]{1,0:T(8,128)(2,1)}, u32[]{:S(2)}) copy-start(bf16[1024,1536]{1,0:T(8,128)(2,1)} %all-gather.11.cloned.1.call-done.k_ref.v_ref) | copy-start | bytes 9437188
  300.3 89.2 %reduce-scatter.5.cloned.1.call-start = ((), (), s32[]{:S(2)}) async-start(), calls=%async_computation.11 | async-start | bytes 3932160 | tf_op jit(solution)/shard_map/reduce_scatter | solution.py:377
  321.2 7.5 %copy-start.16 = (f32[256,768]{1,0:T(8,128)S(1)}, f32[256,768]{1,0:T(8,128)}, u32[]{:S(2)}) copy-start(f32[256,768]{1,0:T(8,128)} %copy-done.15) | copy-start | bytes 2359300
  347.5 8.1 %copy-start.8 = (f32[256,768]{1,0:T(8,128)S(1)}, f32[256,768]{1,0:T(8,128)}, u32[]{:S(2)}) copy-start(f32[256,768]{1,0:T(8,128)} %copy-done.6) | copy-start | bytes 2359300
  347.5 8.1 %copy-start.20 = (f32[256,768]{1,0:T(8,128)S(1)}, f32[256,768]{1,0:T(8,128)}, u32[]{:S(2)}) copy-start(f32[256,768]{1,0:T(8,128)} %copy-done.19) | copy-start | bytes 2359300
  347.5 106.7 %reduce-scatter.11.cloned.1.call-start = ((), (), s32[]{:S(2)}) async-start(), calls=%async_computation.15 | async-start | bytes 5898240 | tf_op jit(solution)/shard_map/reduce_scatter | solution.py:354
  354.6 39.1 %copy-start.22 = (bf16[256,768]{1,0:T(8,128)(2,1)S(1)}, bf16[256,768]{1,0:T(8,128)(2,1)}, u32[]{:S(2)}) copy-start(bf16[256,768]{1,0:T(8,128)(2,1)} %param.13) | copy-start | bytes 1179652
  354.6 39.1 %copy-start.29 = (f32[768]{0:T(1024)S(1)}, f32[768]{0:T(1024)}, u32[]{:S(2)}) copy-start(f32[768]{0:T(1024)} %param.17) | copy-start | bytes 9220
  354.6 156.1 %reduce-scatter.7.cloned.1.call-start = ((), (), s32[]{:S(2)}) async-start(), calls=%async_computation.12 | async-start | bytes 5898240 | tf_op jit(solution)/shard_map/reduce_scatter | solution.py:386
  357.1 39.0 %copy-start.23 = (bf16[768,768]{1,0:T(8,128)(2,1)S(1)}, bf16[768,768]{1,0:T(8,128)(2,1)}, u32[]{:S(2)}) copy-start(bf16[768,768]{1,0:T(8,128)(2,1)} %convolution_convert_fusion.4) | copy-start | bytes 3538948
  399.1 171.8 %reduce-scatter.9.cloned.1.call-start = ((), (), s32[]{:S(2)}) async-start(), calls=%async_computation.14 | async-start | bytes 5898240 | tf_op jit(solution)/shard_map/reduce_scatter | solution.py:351
  405.7 227.1 %all-reduce.5.cloned.1.call-start = ((), (), s32[]{:S(2)}) async-start(), calls=%async_computation.13 | async-start | bytes 2359296 | tf_op jit(solution)/shard_map/psum | solution.py:395
  (19 other events, 75.3 us)
Sparse Core Ops, SparseCore 0:
  9.9 49.9 all-gather.8
  64.3 44.1 all-gather.10
  110.3 27.7 all-gather.12
  139.7 57.0 all-gather.14
  198.5 57.0 all-gather.16
  347.6 41.8 reduce-scatter.4
  392.5 57.9 reduce-scatter.10
  453.5 57.2 reduce-scatter.6
  513.7 57.0 reduce-scatter.8
  573.1 59.6 all-reduce.4

commit v2 on v1

--- a/solution.py
+++ b/solution.py
@@ -220,6 +220,60 @@
     )(qkv_b, kv_all, kv_all, seeds, seg_q, seg_k, attended32, log_rows, grad_attended)
 
 
+def swap(value, axis, mask):
+    count = lax.axis_size(axis)
+    return lax.ppermute(value, axis, [(place, place ^ mask) for place in range(count)])
+
+
+def gather_parts(value, axis, unit, groups):
+    mine = lax.axis_index(axis) // unit
+    whole = jnp.zeros((groups,) + value.shape, value.dtype)
+    whole = lax.dynamic_update_index_in_dim(whole, value, mine, 0)
+    for step in range(1, groups):
+        got = swap(value, axis, step * unit)
+        whole = lax.dynamic_update_index_in_dim(whole, got, mine ^ step, 0)
+    return whole.reshape((groups * value.shape[0],) + value.shape[1:])
+
+
+def scatter_parts(value, axis, unit, groups):
+    mine = lax.axis_index(axis) // unit
+    parts = value.reshape((groups, value.shape[0] // groups) + value.shape[1:])
+    total = lax.dynamic_index_in_dim(parts, mine, 0, False).astype(jnp.float32)
+    for step in range(1, groups):
+        piece = lax.dynamic_index_in_dim(parts, mine ^ step, 0, False)
+        total = total + swap(piece, axis, step * unit).astype(jnp.float32)
+    return total
+
+
+def gather_rows(value, axis):
+    count = lax.axis_size(axis)
+    if count == 4:
+        return gather_parts(value, axis, 1, count)
+    return lax.all_gather(value, axis, axis=0, tiled=True)
+
+
+def scatter_rows(value, axis):
+    count = lax.axis_size(axis)
+    if count == 4:
+        return scatter_parts(value, axis, 1, count)
+    return lax.psum_scatter(value, axis, scatter_dimension=0, tiled=True).astype(jnp.float32)
+
+
+def sum_weights(value):
+    core = lax.axis_index("expert") % 2 == 0
+    stacks = lax.axis_size("expert") // 2
+    half = value.shape[1] // 2
+    left, right = value[:, :half], value[:, half:]
+    mine, other = jnp.where(core, left, right), jnp.where(core, right, left)
+    both = mine.astype(jnp.float32) + swap(other, "expert", 1).astype(jnp.float32)
+    rows = scatter_rows(both.astype(jnp.bfloat16), "shard").astype(jnp.bfloat16)
+    piece = scatter_parts(rows, "expert", 2, stacks).astype(jnp.bfloat16)
+    rows = gather_parts(piece, "expert", 2, stacks)
+    partner = swap(rows, "expert", 1)
+    left, right = jnp.where(core, rows, partner), jnp.where(core, partner, rows)
+    return jnp.concatenate([left, right], axis=1).astype(jnp.float32)
+
+
 def body(
     tokens,
     segments,
@@ -244,14 +298,13 @@
     score_scale = head_size ** (-0.5)
     shard_count = lax.axis_size("shard")
     query_base = lax.axis_index("shard") * rows_here
-    qkv_full, out_full = (
-        lax.all_gather(qkv_weight, "shard", axis=0, tiled=True),
-        lax.all_gather(out_weight, "shard", axis=0, tiled=True),
-    )
-    in_full, out_ff_full = (
-        lax.all_gather(w_in[0], "shard", axis=0, tiled=True),
-        lax.all_gather(w_out[0], "shard", axis=0, tiled=True),
-    )
+    projections = lax.all_gather(
+        jnp.concatenate([qkv_weight, out_weight], axis=1), "shard", axis=0, tiled=True
+    )
+    projections, own_in, own_out = lax.optimization_barrier((projections, w_in[0], w_out[0]))
+    qkv_full, out_full = projections[:, : 3 * width], projections[:, 3 * width :]
+    in_full = lax.all_gather(own_in, "shard", axis=0, tiled=True)
+    out_ff_full = lax.all_gather(own_out, "shard", axis=0, tiled=True)
     inputs32 = tokens.astype(jnp.float32)
     normed_attn, inverse_attn = norm_rows(inputs32, gain_attn)
     normed_attn_b = normed_attn.astype(jnp.bfloat16)
@@ -269,8 +322,8 @@
     offsets_pad = jnp.concatenate([jnp.zeros((heads, 1), jnp.float32), offsets_t], axis=1)
     offsets_here = lax.dynamic_slice_in_dim(offsets_pad, window_first, window, 1)
     seeds = jnp.stack([jnp.roll(offsets_here, row, axis=1) for row in range(8)], axis=1)
-    kv_all = lax.all_gather(key_value, "shard", axis=0, tiled=True)
-    seg_k = lax.all_gather(segments, "shard", axis=0, tiled=True)[None, :]
+    kv_all = gather_rows(key_value, "shard")
+    seg_k = gather_rows(segments, "shard")[None, :]
     seg_q = segments[:, None]
     attended32, log_rows = attend(qkv_b, kv_all, seeds, seg_q, seg_k, head_size)
     attended_b = attended32.astype(jnp.bfloat16)
@@ -298,9 +351,27 @@
     received = lax.all_to_all(send_rows, "expert", split_axis=0, concat_axis=0, tiled=True)
     sources = received.shape[0]
     item_count = received.shape[1]
+    upstream = out_grad.astype(jnp.float32)
+    grad_slots = jnp.dot(
+        dispatch,
+        (gate[:, None] * upstream).astype(jnp.bfloat16),
+        preferred_element_type=jnp.float32,
+    ).astype(jnp.bfloat16)
+    grad_received = lax.all_to_all(
+        grad_slots.reshape(experts, capacity, width),
+        "expert",
+        split_axis=0,
+        concat_axis=0,
+        tiled=True,
+    )
+    grad_flat = grad_received.reshape(-1, width)
     pre = jnp.dot(received.reshape(-1, width), in_full, preferred_element_type=jnp.float32)
-    hidden_ff = jax.nn.gelu(pre, approximate=False).astype(jnp.bfloat16)
-    result = jnp.dot(hidden_ff, out_ff_full, preferred_element_type=jnp.float32).astype(
+    hidden_ff, gelu_back = jax.vjp(partial(jax.nn.gelu, approximate=False), pre)
+    hidden_b = hidden_ff.astype(jnp.bfloat16)
+    grad_out_part = contract_rows(hidden_b, grad_flat).astype(jnp.bfloat16)
+    out_ff_full, grad_out_part = lax.optimization_barrier((out_ff_full, grad_out_part))
+    grad_out_rows = lax.psum_scatter(grad_out_part, "shard", scatter_dimension=0, tiled=True)
+    result = jnp.dot(hidden_b, out_ff_full, preferred_element_type=jnp.float32).astype(
         jnp.bfloat16
     )
     returned_rows = lax.all_to_all(
@@ -310,27 +381,9 @@
         concat_axis=0,
         tiled=True,
     )
-    pre_kept = pre.reshape(sources, item_count, -1)
     expert_out = contract_rows(dispatch, returned_rows.reshape(-1, width))
     output = (hidden1 + gate[:, None] * expert_out).astype(jnp.bfloat16)
-    upstream = out_grad.astype(jnp.float32)
     gate_grad = jnp.sum(upstream * expert_out, axis=1)
-    grad_slots = jnp.dot(
-        dispatch,
-        (gate[:, None] * upstream).astype(jnp.bfloat16),
-        preferred_element_type=jnp.float32,
-    ).astype(jnp.bfloat16)
-    grad_received = lax.all_to_all(
-        grad_slots.reshape(experts, capacity, width),
-        "expert",
-        split_axis=0,
-        concat_axis=0,
-        tiled=True,
-    )
-    grad_flat = grad_received.reshape(-1, width)
-    pre_flat = pre_kept.reshape(grad_flat.shape[0], -1)
-    hidden_ff, gelu_back = jax.vjp(partial(jax.nn.gelu, approximate=False), pre_flat)
-    hidden_b = hidden_ff.astype(jnp.bfloat16)
     grad_hidden = lax.dot_general(
         grad_flat, out_ff_full, (((1,), (1,)), ((), ())), preferred_element_type=jnp.float32
     )
@@ -345,16 +398,9 @@
         concat_axis=0,
         tiled=True,
     )
-    grad_in_part = contract_rows(received.reshape(-1, width), grad_pre)
-    grad_out_part = contract_rows(hidden_b, grad_flat)
-    grad_in_rows, grad_out_rows = (
-        lax.psum_scatter(
-            grad_in_part.astype(jnp.bfloat16), "shard", scatter_dimension=0, tiled=True
-        ).astype(jnp.float32),
-        lax.psum_scatter(
-            grad_out_part.astype(jnp.bfloat16), "shard", scatter_dimension=0, tiled=True
-        ).astype(jnp.float32),
-    )
+    grad_in_part = contract_rows(received.reshape(-1, width), grad_pre).astype(jnp.bfloat16)
+    returned_grad, grad_in_part = lax.optimization_barrier((returned_grad, grad_in_part))
+    grad_in_rows = lax.psum_scatter(grad_in_part, "shard", scatter_dimension=0, tiled=True)
     grad_expert_in = contract_rows(dispatch, returned_grad.reshape(-1, width))
     logit_grad = gate_grad[:, None] * router_probs * (route_onehot - gate[:, None])
     router_grad = contract_rows(normed_moe, logit_grad, highest)
@@ -371,10 +417,11 @@
     grad_attended = lax.dot_general(
         branch_grad, out_full, (((1,), (1,)), ((), ())), preferred_element_type=jnp.float32
     ).astype(jnp.bfloat16)
+    grad_attended, grad_out_rows = lax.optimization_barrier((grad_attended, grad_out_rows))
     query_grad, pair_grads, seed_grads = attend_back(
         qkv_b, kv_all, seeds, seg_q, seg_k, attended32, log_rows, grad_attended, head_size
     )
-    kv_grad = lax.psum_scatter(pair_grads, "shard", scatter_dimension=0, tiled=True)
+    kv_grad = scatter_rows(pair_grads, "shard").astype(jnp.bfloat16)
     kv_grad = kv_grad.reshape(rows_here, heads // 2, 2, 2 * head_size)
     kv_grad = kv_grad.transpose(0, 2, 1, 3).reshape(rows_here, 2 * width)
     grad_qkv_b = jnp.concatenate([query_grad, kv_grad], axis=1)
@@ -383,16 +430,11 @@
     )
     grad_attn_in, gain_attn_grad = norm_back(inputs32, inverse_attn, gain_attn, grad_normed_attn)
     grad_tokens = grad_hidden1 + grad_attn_in
-    weight_rows = lax.psum_scatter(
-        jnp.concatenate(
-            [contract_rows(normed_attn_b, grad_qkv_b), contract_rows(attended_b, branch_grad)],
-            axis=1,
-        ).astype(jnp.bfloat16),
-        "shard",
-        scatter_dimension=0,
-        tiled=True,
-    ).astype(jnp.float32)
-    weight_rows = lax.psum(weight_rows.astype(jnp.bfloat16), "expert").astype(jnp.float32)
+    weight_part = jnp.concatenate(
+        [contract_rows(normed_attn_b, grad_qkv_b), contract_rows(attended_b, branch_grad)], axis=1
+    ).astype(jnp.bfloat16)
+    weight_part, grad_in_rows = lax.optimization_barrier((weight_part, grad_in_rows))
+    weight_rows = sum_weights(weight_part)
     window_grad = sum(jnp.roll(seed_grads[:, row], -row, axis=1) for row in range(8))
     onehot_pad = jnp.concatenate([jnp.zeros_like(bucket_onehot[:1]), bucket_onehot], axis=0)
     onehot_here = lax.dynamic_slice_in_dim(onehot_pad, window_first, window, 0)
@@ -411,8 +453,8 @@
         router_total,
         weight_rows[:, : 3 * width],
         weight_rows[:, 3 * width :],
-        grad_in_rows[None],
-        grad_out_rows[None],
+        grad_in_rows.astype(jnp.float32)[None],
+        grad_out_rows.astype(jnp.float32)[None],
     )
 
 

time: 651 us -> 510 us (0.78)
  waiting for transfers between devices: 418 us -> 237 us
  starting transfers between devices: 18.7 us -> 43 us
  other arithmetic: 15 us -> 25.5 us
  blocking collectives: 49.2 us -> 38.8 us
  local copies, waits for them, and re-layouts: 21.4 us -> 31.6 us
    reduce_scatter x4 -> x2, waiting for transfers between devices: 146 us -> 0.01 us  [the longest x1 0.01 us: body(): lax.psum_scatter(grad_out_part, 'shard', scatter_dimension=0, tiled=True)]
    ppermute x0 -> x20, waiting for transfers between devices: none -> 125 us  [swap(): lax.ppermute(value, axis, [(place, place ^ mask) for place in range(count)])]
    all_gather x5 -> x3, waiting for transfers between devices: 161 us -> 60.5 us  [the longest x1 60.5 us: body(): lax.all_gather(jnp.concatenate([qkv_weight, out_weight], axis=1), 'shard'...]
    psum x1 -> x0, waiting for transfers between devices: 58.9 us -> none  [body(): lax.psum(weight_rows.astype(jnp.bfloat16), 'expert').astype(jnp.float32)]
    ppermute x0 -> x20, starting transfers between devices: none -> 25.2 us  [swap(): lax.ppermute(value, axis, [(place, place ^ mask) for place in range(count)])]
    dynamic_slice x0 -> x4, local copies, waits for them, and re-layouts: none -> 8.55 us  [the longest x3 7.06 us: scatter_parts(): piece = lax.dynamic_index_in_dim(parts, mine ^ step, 0, False)]
    all_gather x1 -> x0, blocking collectives: 8.03 us -> none  [body(): seg_k = lax.all_gather(segments, 'shard', axis=0, tiled=True)[None, :]]
    convert_element_type x0 -> x4, other arithmetic: none -> 6.63 us  [the longest x2 4.31 us: sum_weights(): rows = scatter_rows(both.astype(jnp.bfloat16), 'shard').astype(jnp.bfloat16)]
  transfers between devices with their start and end apart: 14 -> 29, of which waited for: 12 -> 16; matrix products, arithmetic and copies ran while one was open for 12% -> 24% of each run, Pallas kernels for 2% -> 5%
where the time goes in v2:
time: 510 us; the launch traced here: 503 us
  waiting for transfers between devices  237 us (46%)
  matrix products  84.7 us (17%)
  starting transfers between devices  43 us (8%)
  blocking collectives  38.8 us (8%)
  local copies, waits for them, and re-layouts  31.6 us (6%)
  Pallas kernels  27.2 us (5%)
  other arithmetic  25.5 us (5%)
  between operations  15.2 us (3%)
    ppermute x20, waiting for transfers between devices, swap(): lax.ppermute(value, axis, [(place, place ^ mask) for place in range(count)])  125 us
    all_gather x1, waiting for transfers between devices, body(): lax.all_gather(jnp.concatenate([qkv_weight, out_weight], axis=1), 'shard'...  60.5 us
    psum x1, blocking collectives, body(): lax.psum((gain_attn_grad, gain_moe_grad, table_grad, router_grad), ('expe...  38.8 us
    ppermute x20, starting transfers between devices, swap(): lax.ppermute(value, axis, [(place, place ^ mask) for place in range(count)])  25.2 us
    dot_general x7, matrix products, contract_rows(): lax.dot_general(left, right, (((0,), (0,)), ((), ())), precision=precisio...  21.7 us
    dot_general x1, matrix products, body(): jnp.dot(received.reshape(-1, width), in_full, preferred_element_type=jnp....  18.8 us
    all_to_all x1, waiting for transfers between devices, body(): lax.all_to_all(result.reshape(sources, item_count, width), 'expert', spli...  18.5 us
    all_to_all x1, waiting for transfers between devices, body(): lax.all_to_all(send_rows, 'expert', split_axis=0, concat_axis=0, tiled=True)  16.7 us
  transfers between devices with their start and end apart: 29, of which 16 were waited for; matrix products, arithmetic and copies ran while one was open for 24% of the time, Pallas kernels for 5%

profile of v2, /device:TPU:0, one launch (start us, length us, event | category | flops | bytes accessed | tf_op | source)
XLA Modules:
  0.0 502.6 jit_solution(4670746415212153839)
XLA Ops:
  9.8 60.5 %all-gather.4.cloned.1.call-done = bf16[768,3072]{1,0:T(8,128)(2,1)} async-done(((bf16[192,3072]{1,0:T(8,128)(2,1)}), bf16[768,3072]{1,0:T(8,128)(2,1)}) %all-gather.4.cloned.1.call-update) | async-done | bytes 4718608 | tf_op jit(solution)/shard_map/all_gather | solution.py:301
  77.8 3.6 convolution_convert_fusion.3.q_ref
  91.1 22.1 %collective-permute-done = bf16[256,1536]{1,0:T(8,128)(2,1)} collective-permute-done((bf16[256,1536]{1,0:T(8,128)(2,1)}, bf16[256,1536]{1,0:T(8,128)(2,1)}, u32[]{:S(2)}, u32[]{:S(2)}) %collective-permute-start) | collective-permute-done | bytes 786464 | tf_op jit(solution)/shard_map/ppermute | solution.py:225
  115.6 31.0 %collective-permute-done.2 = bf16[256,1536]{1,0:T(8,128)(2,1)} collective-permute-done((bf16[256,1536]{1,0:T(8,128)(2,1)}, bf16[256,1536]{1,0:T(8,128)(2,1)}, u32[]{:S(2)}, u32[]{:S(2)}) %collective-permute-start.2) | collective-permute-done | bytes 786464 | tf_op jit(solution)/shard_map/ppermute | solution.py:225
  147.8 11.5 %shard_map.204 = (f32[256,768]{1,0:T(8,128)S(1)}, f32[256,768]{1,0:T(8,128)S(1)}) custom-call(bf16[256,2304]{1,0:T(8,128)(2,1)S(1)} %copy-done.2, bf16[1024,1536]{1,0:T(8,128)(2,1)S(1)} %bitcast.145, bf16[1024,1536]{1,0:T(8,128)(2,1)S(1)} %bitcast.146, f32[12,8,1280]{2,1,0:T(8,128)S(1)} %copy-done.7, s32[256,1]{1,0:T(8,128)S(1)} %copy.60.segq_ref, ...), custom_call_target="tpu_custom_call" | custom-call | flops 1610612736 | bytes 5111808 | tf_op jit(solution)/shard_map/pallas_call | solution.py:174
  164.6 4.5 all-to-all-start
  173.5 16.7 %all-to-all-done = bf16[8,64,768]{2,1,0:T(8,128)(2,1)} async-done(((bf16[8,64,768]{2,1,0:T(8,128)(2,1)}), bf16[8,64,768]{2,1,0:T(8,128)(2,1)}, u32[]{:S(2)}, u32[]{:S(2)}) %all-to-all-start) | async-done | bytes 786464 | tf_op jit(solution)/shard_map/all_to_all | solution.py:351
  190.2 4.2 all-to-all-start.1
  194.7 18.8 %multiply_convert_fusion = (bf16[512,3072]{1,0:T(8,128)(2,1)}, f32[512,3072]{1,0:T(8,128)}, f32[512,3072]{1,0:T(8,128)}) fusion(bf16[512,768]{1,0:T(8,128)(2,1)} %bitcast.24, bf16[768,3072]{1,0:T(8,128)(2,1)} %all-gather.6.cloned.1.call-done), kind=kOutput, calls=%fused_computation.3 | convolution fusion | flops 2518155264 | bytes 21233664 | tf_op jit(solution)/shard_map/dot_general | solution.py:368
  215.4 7.0 %convolution_convert_fusion.2 = bf16[3072,768]{1,0:T(8,128)(2,1)} fusion(bf16[512,3072]{1,0:T(8,128)(2,1)} %get-tuple-element.52, bf16[512,768]{1,0:T(8,128)(2,1)} %bitcast.26), kind=kOutput, calls=%fused_computation.19 | convolution fusion | flops 2418278400 | bytes 8650752 | tf_op jit(solution)/shard_map/dot_general | solution.py:32
  222.4 11.0 %add_convert_fusion = bf16[512,3072]{1,0:T(8,128)(2,1)S(1)} fusion(f32[512,3072]{1,0:T(8,128)} %get-tuple-element.53, f32[512,3072]{1,0:T(8,128)} %get-tuple-element.82, bf16[512,768]{1,0:T(8,128)(2,1)} %bitcast.26, bf16[3072,768]{1,0:T(8,128)(2,1)} %all-gather.8.cloned.1.call-done), kind=kOutput, calls=%fused_computation.2 | convolution fusion | flops 2437939200 | bytes 21233664 | tf_op jit(solution)/shard_map/dot_general | solution.py:387
  233.4 7.1 %convolution_convert_fusion.5 = bf16[512,768]{1,0:T(8,128)(2,1)} fusion(bf16[512,3072]{1,0:T(8,128)(2,1)S(1)} %add_convert_fusion, bf16[768,3072]{1,0:T(8,128)(2,1)} %all-gather.6.cloned.1.call-done), kind=kOutput, calls=%fused_computation.39 | convolution fusion | flops 2416312320 | bytes 8650752 | tf_op jit(solution)/shard_map/dot_general | solution.py:391
  240.5 4.5 all-to-all-start.3
  245.0 7.0 %convolution_convert_fusion.1 = bf16[768,3072]{1,0:T(8,128)(2,1)} fusion(bf16[512,768]{1,0:T(8,128)(2,1)} %bitcast.24, bf16[512,3072]{1,0:T(8,128)(2,1)} %copy-done.35), kind=kOutput, calls=%fused_computation.18 | convolution fusion | flops 2418278400 | bytes 8650752 | tf_op jit(solution)/shard_map/dot_general | solution.py:32
  252.1 13.9 %all-to-all-done.3 = bf16[8,64,768]{2,1,0:T(8,128)(2,1)} async-done(((bf16[8,64,768]{2,1,0:T(8,128)(2,1)}), bf16[8,64,768]{2,1,0:T(8,128)(2,1)}, u32[]{:S(2)}, u32[]{:S(2)}) %all-to-all-start.3) | async-done | bytes 786464 | tf_op jit(solution)/shard_map/all_to_all | solution.py:394
  266.0 6.9 %convolution_convert_fusion.6 = bf16[512,768]{1,0:T(8,128)(2,1)} fusion(bf16[512,3072]{1,0:T(8,128)(2,1)} %get-tuple-element.52, bf16[3072,768]{1,0:T(8,128)(2,1)} %all-gather.8.cloned.1.call-done), kind=kOutput, calls=%fused_computation.40 | convolution fusion | flops 2416312320 | bytes 8650752 | tf_op jit(solution)/shard_map/dot_general | solution.py:374
  272.9 4.2 all-to-all-start.2
  279.5 18.5 %all-to-all-done.2 = bf16[8,64,768]{2,1,0:T(8,128)(2,1)} async-done(((bf16[8,64,768]{2,1,0:T(8,128)(2,1)}), bf16[8,64,768]{2,1,0:T(8,128)(2,1)}, u32[]{:S(2)}, u32[]{:S(2)}) %all-to-all-start.2) | async-done | bytes 786464 | tf_op jit(solution)/shard_map/all_to_all | solution.py:377
  299.9 2.5 multiply_reduce_fusion
  305.4 2.6 convolution_convert_fusion.9.grad_ref
  313.5 15.8 %shard_map.205 = (bf16[256,768]{1,0:T(8,128)(2,1)S(1)}, bf16[1024,1536]{1,0:T(8,128)(2,1)S(1)}, f32[12,8,1280]{2,1,0:T(8,128)S(1)}) custom-call(bf16[256,2304]{1,0:T(8,128)(2,1)S(1)} %copy-done.3, bf16[1024,1536]{1,0:T(8,128)(2,1)S(1)} %bitcast.147, bf16[1024,1536]{1,0:T(8,128)(2,1)S(1)} %bitcast.148, f32[12,8,1280]{2,1,0:T(8,128)S(1)} %copy-done.8, ...), custom_call_target="tpu_custom_call" | custom-call | flops 4026531840 | bytes 9043968 | tf_op jit(solution)/shard_map/pallas_call | solution.py:194
  338.6 2.9 collective-permute-start.8
  344.3 9.9 %collective-permute-done.6 = bf16[256,1536]{0,1:T(8,128)(2,1)} collective-permute-done((bf16[256,1536]{0,1:T(8,128)(2,1)}, bf16[256,1536]{0,1:T(8,128)(2,1)}, u32[]{:S(2)}, u32[]{:S(2)}) %collective-permute-start.6) | collective-permute-done | bytes 786464 | tf_op jit(solution)/shard_map/ppermute | solution.py:225
  354.2 17.8 %collective-permute-done.7 = bf16[256,1536]{0,1:T(8,128)(2,1)} collective-permute-done((bf16[256,1536]{0,1:T(8,128)(2,1)}, bf16[256,1536]{0,1:T(8,128)(2,1)}, u32[]{:S(2)}, u32[]{:S(2)}) %collective-permute-start.7) | collective-permute-done | bytes 786464 | tf_op jit(solution)/shard_map/ppermute | solution.py:225
  375.5 2.8 pad_maximum_fusion
  378.3 4.1 broadcast_select_fusion
  387.3 4.0 add_convert_fusion.1
  396.9 10.8 %collective-permute-done.10 = bf16[192,1536]{1,0:T(8,128)(2,1)S(1)} collective-permute-done((bf16[192,1536]{1,0:T(8,128)(2,1)S(1)}, bf16[192,1536]{1,0:T(8,128)(2,1)S(1)}, u32[]{:S(2)}, u32[]{:S(2)}) %collective-permute-start.10) | collective-permute-done | bytes 589856 | tf_op jit(solution)/shard_map/ppermute | solution.py:225
  407.7 13.3 %collective-permute-done.11 = bf16[192,1536]{1,0:T(8,128)(2,1)S(1)} collective-permute-done((bf16[192,1536]{1,0:T(8,128)(2,1)S(1)}, bf16[192,1536]{1,0:T(8,128)(2,1)S(1)}, u32[]{:S(2)}, u32[]{:S(2)}) %collective-permute-start.11) | collective-permute-done | bytes 589856 | tf_op jit(solution)/shard_map/ppermute | solution.py:225
  428.0 7.0 %collective-permute-done.14 = bf16[48,1536]{1,0:T(8,128)(2,1)S(1)} collective-permute-done((bf16[48,1536]{1,0:T(8,128)(2,1)S(1)}, bf16[48,1536]{1,0:T(8,128)(2,1)S(1)}, u32[]{:S(2)}, u32[]{:S(2)}) %collective-permute-start.14) | collective-permute-done | bytes 147488 | tf_op jit(solution)/shard_map/ppermute | solution.py:225
  438.6 38.8 %all-reduce.2 = (f32[768]{0:T(1024)}, f32[768]{0:T(1024)}, f32[32,12]{0,1:T(8,128)}, f32[768,8]{0,1:T(8,128)}) all-reduce(f32[768]{0:T(1024)S(1)} %get-tuple-element.44, f32[768]{0:T(1024)S(1)} %get-tuple-element.42, f32[32,12]{0,1:T(8,128)S(1)} %fusion.28, ...), channel_id=1, replica_groups=mesh['expert'=8,'shard'=4] {'expert','shard'}, use_global_device_ids=true, to_apply=%region_13.14 | all-reduce | flops 8064 | bytes 64512 | tf_op jit(solution)/shard_map/psum | solution.py:444
  481.8 9.2 %collective-permute-done.17 = bf16[48,1536]{1,0:T(8,128)(2,1)S(1)} collective-permute-done((bf16[48,1536]{1,0:T(8,128)(2,1)S(1)}, bf16[48,1536]{1,0:T(8,128)(2,1)S(1)}, u32[]{:S(2)}, u32[]{:S(2)}) %collective-permute-start.17) | collective-permute-done | bytes 147488 | tf_op jit(solution)/shard_map/ppermute | solution.py:225
  (237 shorter events, 93.0 us)
Async XLA Ops:
  7.2 161.9 %copy-start = (f32[768,8]{0,1:T(8,128)S(1)}, f32[768,8]{0,1:T(8,128)}, u32[]{:S(2)}) copy-start(f32[768,8]{0,1:T(8,128)} %param.20) | copy-start | bytes 73732
  7.2 70.6 %copy-start.29 = (f32[768]{0:T(1024)S(1)}, f32[768]{0:T(1024)}, u32[]{:S(2)}) copy-start(f32[768]{0:T(1024)} %param.17) | copy-start | bytes 9220
  7.3 63.0 %all-gather.4.cloned.1.call-start = ((), (), s32[]{:S(2)}) async-start(), calls=%async_computation.6 | async-start | bytes 5898240 | tf_op jit(solution)/shard_map/all_gather | solution.py:301
  9.8 184.9 %all-gather.6.cloned.1.call-start = ((), (), s32[]{:S(2)}) async-start(), calls=%async_computation.7 | async-start | bytes 5898240 | tf_op jit(solution)/shard_map/all_gather | solution.py:306
  70.3 152.0 %all-gather.8.cloned.1.call-start = ((), (), s32[]{:S(2)}) async-start(), calls=%async_computation.8 | async-start | bytes 5898240 | tf_op jit(solution)/shard_map/all_gather | solution.py:307
  70.4 16.8 %collective-permute-start.3 = (s32[256]{0:T(256)S(1)}, s32[256]{0:T(256)S(1)}, u32[]{:S(2)}, u32[]{:S(2)}) collective-permute-start(s32[256]{0:T(256)S(1)} %copy-done.33), channel_id=1, source_target_pairs={{0,1},{1,0},{2,3},{3,2},{4,5},{5,4},{6,7},{7,6},{8,9},{9,8},{10,11... | collective-permute-start | bytes 3080 | tf_op jit(solution)/shard_map/ppermute | solution.py:225
  71.9 15.3 %collective-permute-start.4 = (s32[256]{0:T(256)S(1)}, s32[256]{0:T(256)S(1)}, u32[]{:S(2)}, u32[]{:S(2)}) collective-permute-start(s32[256]{0:T(256)S(1)} %copy-done.33), channel_id=1, source_target_pairs={{0,2},{1,3},{2,0},{3,1},{4,6},{5,7},{6,4},{7,5},{8,10},{9,11},{10,... | collective-permute-start | bytes 3080 | tf_op jit(solution)/shard_map/ppermute | solution.py:225
  72.5 14.8 %collective-permute-start.5 = (s32[256]{0:T(256)S(1)}, s32[256]{0:T(256)S(1)}, u32[]{:S(2)}, u32[]{:S(2)}) collective-permute-start(s32[256]{0:T(256)S(1)} %copy-done.33), channel_id=1, source_target_pairs={{0,3},{1,2},{2,1},{3,0},{4,7},{5,6},{6,5},{7,4},{8,11},{9,10},{10,... | collective-permute-start | bytes 3080 | tf_op jit(solution)/shard_map/ppermute | solution.py:225
  83.4 29.8 %collective-permute-start = (bf16[256,1536]{1,0:T(8,128)(2,1)}, bf16[256,1536]{1,0:T(8,128)(2,1)}, u32[]{:S(2)}, u32[]{:S(2)}) collective-permute-start(bf16[256,1536]{1,0:T(8,128)(2,1)} %slice.208), channel_id=1, source_target_pairs={{0,1},{1,0},{2,3},{3,2},{4,5},{5,4},{6,7},{7,6},{8,9},{9,8},{10,11... | collective-permute-start | bytes 2359304 | tf_op jit(solution)/shard_map/ppermute | solution.py:225
  87.3 27.1 %collective-permute-start.1 = (bf16[256,1536]{1,0:T(8,128)(2,1)}, bf16[256,1536]{1,0:T(8,128)(2,1)}, u32[]{:S(2)}, u32[]{:S(2)}) collective-permute-start(bf16[256,1536]{1,0:T(8,128)(2,1)} %slice.208), channel_id=1, source_target_pairs={{0,2},{1,3},{2,0},{3,1},{4,6},{5,7},{6,4},{7,5},{8,10},{9,11},{10,... | collective-permute-start | bytes 2359304 | tf_op jit(solution)/shard_map/ppermute | solution.py:225
  87.6 59.0 %collective-permute-start.2 = (bf16[256,1536]{1,0:T(8,128)(2,1)}, bf16[256,1536]{1,0:T(8,128)(2,1)}, u32[]{:S(2)}, u32[]{:S(2)}) collective-permute-start(bf16[256,1536]{1,0:T(8,128)(2,1)} %slice.208), channel_id=1, source_target_pairs={{0,3},{1,2},{2,1},{3,0},{4,7},{5,6},{6,5},{7,4},{8,11},{9,10},{10,... | collective-permute-start | bytes 2359304 | tf_op jit(solution)/shard_map/ppermute | solution.py:225
  164.6 25.6 %all-to-all-start = ((bf16[8,64,768]{2,1,0:T(8,128)(2,1)}), bf16[8,64,768]{2,1,0:T(8,128)(2,1)}, u32[]{:S(2)}, u32[]{:S(2)}) async-start(bf16[8,64,768]{2,1,0:T(8,128)(2,1)} %bitcast.155), calls=%async_computation | async-start | bytes 1572864 | tf_op jit(solution)/shard_map/all_to_all | solution.py:351
  190.2 25.2 %all-to-all-start.1 = ((bf16[8,64,768]{2,1,0:T(8,128)(2,1)}), bf16[8,64,768]{2,1,0:T(8,128)(2,1)}, u32[]{:S(2)}, u32[]{:S(2)}) async-start(bf16[8,64,768]{2,1,0:T(8,128)(2,1)} %bitcast.154), calls=%async_computation.1 | async-start | bytes 1572864 | tf_op jit(solution)/shard_map/all_to_all | solution.py:360
  194.4 113.5 %reduce-scatter.3.cloned.1.call-start = ((), (), s32[]{:S(2)}) async-start(), calls=%async_computation.9 | async-start | bytes 5898240 | tf_op jit(solution)/shard_map/reduce_scatter | solution.py:373
  240.5 25.5 %all-to-all-start.3 = ((bf16[8,64,768]{2,1,0:T(8,128)(2,1)}), bf16[8,64,768]{2,1,0:T(8,128)(2,1)}, u32[]{:S(2)}, u32[]{:S(2)}) async-start(bf16[8,64,768]{2,1,0:T(8,128)(2,1)} %bitcast.169), calls=%async_computation.3 | async-start | bytes 1572864 | tf_op jit(solution)/shard_map/all_to_all | solution.py:394
  245.0 133.4 %reduce-scatter.5.cloned.1.call-start = ((), (), s32[]{:S(2)}) async-start(), calls=%async_computation.10 | async-start | bytes 5898240 | tf_op jit(solution)/shard_map/reduce_scatter | solution.py:403
  272.9 25.2 %all-to-all-start.2 = ((bf16[8,64,768]{2,1,0:T(8,128)(2,1)}), bf16[8,64,768]{2,1,0:T(8,128)(2,1)}, u32[]{:S(2)}, u32[]{:S(2)}) async-start(bf16[8,64,768]{2,1,0:T(8,128)(2,1)} %bitcast.170), calls=%async_computation.2 | async-start | bytes 1572864 | tf_op jit(solution)/shard_map/all_to_all | solution.py:377
  333.4 20.8 %collective-permute-start.6 = (bf16[256,1536]{0,1:T(8,128)(2,1)}, bf16[256,1536]{0,1:T(8,128)(2,1)}, u32[]{:S(2)}, u32[]{:S(2)}) collective-permute-start(bf16[256,1536]{0,1:T(8,128)(2,1)} %bitcast.166), channel_id=1, source_target_pairs={{0,1},{1,0},{2,3},{3,2},{4,5},{5,4},{6,7},{7,6},{8,9},{9,8},{10,11... | collective-permute-start | bytes 2359304 | tf_op jit(solution)/shard_map/ppermute | solution.py:225
  335.9 36.1 %collective-permute-start.7 = (bf16[256,1536]{0,1:T(8,128)(2,1)}, bf16[256,1536]{0,1:T(8,128)(2,1)}, u32[]{:S(2)}, u32[]{:S(2)}) collective-permute-start(bf16[256,1536]{0,1:T(8,128)(2,1)} %bitcast.167), channel_id=1, source_target_pairs={{0,2},{1,3},{2,0},{3,1},{4,6},{5,7},{6,4},{7,5},{8,10},{9,11},{10,... | collective-permute-start | bytes 2359304 | tf_op jit(solution)/shard_map/ppermute | solution.py:225
  338.6 33.4 %collective-permute-start.8 = (bf16[256,1536]{0,1:T(8,128)(2,1)}, bf16[256,1536]{0,1:T(8,128)(2,1)}, u32[]{:S(2)}, u32[]{:S(2)}) collective-permute-start(bf16[256,1536]{0,1:T(8,128)(2,1)} %bitcast.168), channel_id=1, source_target_pairs={{0,3},{1,2},{2,1},{3,0},{4,7},{5,6},{6,5},{7,4},{8,11},{9,10},{10,... | collective-permute-start | bytes 2359304 | tf_op jit(solution)/shard_map/ppermute | solution.py:225
  382.4 4.9 collective-permute-start.9
  391.5 16.2 %collective-permute-start.10 = (bf16[192,1536]{1,0:T(8,128)(2,1)S(1)}, bf16[192,1536]{1,0:T(8,128)(2,1)S(1)}, u32[]{:S(2)}, u32[]{:S(2)}) collective-permute-start(bf16[192,1536]{1,0:T(8,128)(2,1)S(1)} %get-tuple-element.58), channel_id=1, source_target_pairs={{0,1},{1,0},{2,3},{3,2},{4,5},{5,4},{6,7},{7,6},{8,9},{9,8},{10,11... | collective-permute-start | bytes 1769480 | tf_op jit(solution)/shard_map/ppermute | solution.py:225
  393.3 27.7 %collective-permute-start.11 = (bf16[192,1536]{1,0:T(8,128)(2,1)S(1)}, bf16[192,1536]{1,0:T(8,128)(2,1)S(1)}, u32[]{:S(2)}, u32[]{:S(2)}) collective-permute-start(bf16[192,1536]{1,0:T(8,128)(2,1)S(1)} %get-tuple-element.60), channel_id=1, source_target_pairs={{0,2},{1,3},{2,0},{3,1},{4,6},{5,7},{6,4},{7,5},{8,10},{9,11},{10,... | collective-permute-start | bytes 1769480 | tf_op jit(solution)/shard_map/ppermute | solution.py:225
  393.8 27.2 %collective-permute-start.12 = (bf16[192,1536]{1,0:T(8,128)(2,1)S(1)}, bf16[192,1536]{1,0:T(8,128)(2,1)S(1)}, u32[]{:S(2)}, u32[]{:S(2)}) collective-permute-start(bf16[192,1536]{1,0:T(8,128)(2,1)S(1)} %get-tuple-element.59), channel_id=1, source_target_pairs={{0,3},{1,2},{2,1},{3,0},{4,7},{5,6},{6,5},{7,4},{8,11},{9,10},{10,... | collective-permute-start | bytes 1769480 | tf_op jit(solution)/shard_map/ppermute | solution.py:225
  396.9 94.2 %copy-start.27 = (bf16[192,3072]{1,0:T(8,128)(2,1)S(1)}, bf16[192,3072]{1,0:T(8,128)(2,1)}, u32[]{:S(2)}) copy-start(bf16[192,3072]{1,0:T(8,128)(2,1)} %reduce-scatter.5.cloned.1.call-done) | copy-start | bytes 3538948
  421.3 6.7 %collective-permute-start.13 = (bf16[48,1536]{1,0:T(8,128)(2,1)S(1)}, bf16[48,1536]{1,0:T(8,128)(2,1)S(1)}, u32[]{:S(2)}, u32[]{:S(2)}) collective-permute-start(bf16[48,1536]{1,0:T(8,128)(2,1)S(1)} %get-tuple-element.71), channel_id=1, source_target_pairs={{0,8},{4,12},{8,0},{12,4},{16,24},{20,28},{24,16},{28,20},{1,9},{5... | collective-permute-start | bytes 442376 | tf_op jit(solution)/shard_map/ppermute | solution.py:225
  421.4 13.6 %collective-permute-start.14 = (bf16[48,1536]{1,0:T(8,128)(2,1)S(1)}, bf16[48,1536]{1,0:T(8,128)(2,1)S(1)}, u32[]{:S(2)}, u32[]{:S(2)}) collective-permute-start(bf16[48,1536]{1,0:T(8,128)(2,1)S(1)} %get-tuple-element.73), channel_id=1, source_target_pairs={{0,16},{4,20},{8,24},{12,28},{16,0},{20,4},{24,8},{28,12},{1,17},{... | collective-permute-start | bytes 442376 | tf_op jit(solution)/shard_map/ppermute | solution.py:225
  423.6 11.4 %collective-permute-start.15 = (bf16[48,1536]{1,0:T(8,128)(2,1)S(1)}, bf16[48,1536]{1,0:T(8,128)(2,1)S(1)}, u32[]{:S(2)}, u32[]{:S(2)}) collective-permute-start(bf16[48,1536]{1,0:T(8,128)(2,1)S(1)} %get-tuple-element.72), channel_id=1, source_target_pairs={{0,24},{4,28},{8,16},{12,20},{16,8},{20,12},{24,0},{28,4},{1,25},{... | collective-permute-start | bytes 442376 | tf_op jit(solution)/shard_map/ppermute | solution.py:225
  435.2 46.6 %collective-permute-start.16 = (bf16[48,1536]{1,0:T(8,128)(2,1)S(1)}, bf16[48,1536]{1,0:T(8,128)(2,1)S(1)}, u32[]{:S(2)}, u32[]{:S(2)}) collective-permute-start(bf16[48,1536]{1,0:T(8,128)(2,1)S(1)} %get-tuple-element.51), channel_id=1, source_target_pairs={{0,8},{4,12},{8,0},{12,4},{16,24},{20,28},{24,16},{28,20},{1,9},{5... | collective-permute-start | bytes 442376 | tf_op jit(solution)/shard_map/ppermute | solution.py:225
  477.4 13.6 %collective-permute-start.17 = (bf16[48,1536]{1,0:T(8,128)(2,1)S(1)}, bf16[48,1536]{1,0:T(8,128)(2,1)S(1)}, u32[]{:S(2)}, u32[]{:S(2)}) collective-permute-start(bf16[48,1536]{1,0:T(8,128)(2,1)S(1)} %get-tuple-element.51), channel_id=1, source_target_pairs={{0,16},{4,20},{8,24},{12,28},{16,0},{20,4},{24,8},{28,12},{1,17},{... | collective-permute-start | bytes 442376 | tf_op jit(solution)/shard_map/ppermute | solution.py:225
  479.5 11.5 %collective-permute-start.18 = (bf16[48,1536]{1,0:T(8,128)(2,1)S(1)}, bf16[48,1536]{1,0:T(8,128)(2,1)S(1)}, u32[]{:S(2)}, u32[]{:S(2)}) collective-permute-start(bf16[48,1536]{1,0:T(8,128)(2,1)S(1)} %get-tuple-element.51), channel_id=1, source_target_pairs={{0,24},{4,28},{8,16},{12,20},{16,8},{20,12},{24,0},{28,4},{1,25},{... | collective-permute-start | bytes 442376 | tf_op jit(solution)/shard_map/ppermute | solution.py:225
  491.0 2.1 collective-permute-start.19
  (35 other events, 678.0 us)
Sparse Core Ops, SparseCore 0:
  10.5 59.7 all-gather.3
  72.1 83.2 all-gather.5
  157.3 56.9 all-gather.7
  222.5 54.6 reduce-scatter.2
  280.0 57.0 reduce-scatter.4

commit v3 on v2

--- a/solution.py
+++ b/solution.py
@@ -259,6 +259,15 @@
     return lax.psum_scatter(value, axis, scatter_dimension=0, tiled=True).astype(jnp.float32)
 
 
+def gather_halves(value):
+    core = lax.axis_index("expert") % 2 == 0
+    half = value.shape[1] // 2
+    mine = gather_rows(jnp.where(core, value[:, :half], value[:, half:]), "shard")
+    partner = swap(mine, "expert", 1)
+    left, right = jnp.where(core, mine, partner), jnp.where(core, partner, mine)
+    return jnp.concatenate([left, right], axis=1)
+
+
 def sum_weights(value):
     core = lax.axis_index("expert") % 2 == 0
     stacks = lax.axis_size("expert") // 2
@@ -298,9 +307,7 @@
     score_scale = head_size ** (-0.5)
     shard_count = lax.axis_size("shard")
     query_base = lax.axis_index("shard") * rows_here
-    projections = lax.all_gather(
-        jnp.concatenate([qkv_weight, out_weight], axis=1), "shard", axis=0, tiled=True
-    )
+    projections = gather_halves(jnp.concatenate([qkv_weight, out_weight], axis=1))
     projections, own_in, own_out = lax.optimization_barrier((projections, w_in[0], w_out[0]))
     qkv_full, out_full = projections[:, : 3 * width], projections[:, 3 * width :]
     in_full = lax.all_gather(own_in, "shard", axis=0, tiled=True)
@@ -391,6 +398,7 @@
     grad_back_rows = lax.dot_general(
         grad_pre, in_full, (((1,), (1,)), ((), ())), preferred_element_type=jnp.float32
     ).astype(jnp.bfloat16)
+    grad_back_rows, returned_rows = lax.optimization_barrier((grad_back_rows, returned_rows))
     returned_grad = lax.all_to_all(
         grad_back_rows.reshape(grad_received.shape),
         "expert",
@@ -403,7 +411,7 @@
     grad_in_rows = lax.psum_scatter(grad_in_part, "shard", scatter_dimension=0, tiled=True)
     grad_expert_in = contract_rows(dispatch, returned_grad.reshape(-1, width))
     logit_grad = gate_grad[:, None] * router_probs * (route_onehot - gate[:, None])
-    router_grad = contract_rows(normed_moe, logit_grad, highest)
+    router_grad = contract_rows(logit_grad, normed_moe, highest)
     grad_normed_moe = grad_expert_in + lax.dot_general(
         logit_grad,
         router_weight,
@@ -439,11 +447,16 @@
     onehot_pad = jnp.concatenate([jnp.zeros_like(bucket_onehot[:1]), bucket_onehot], axis=0)
     onehot_here = lax.dynamic_slice_in_dim(onehot_pad, window_first, window, 0)
     table_grad = jnp.dot(
-        window_grad, onehot_here, precision=highest, preferred_element_type=jnp.float32
-    ).T
-    gain_attn_total, gain_moe_total, table_total, router_total = lax.psum(
-        (gain_attn_grad, gain_moe_grad, table_grad, router_grad), ("expert", "shard")
-    )
+        onehot_here.T, window_grad.T, precision=highest, preferred_element_type=jnp.float32
+    )
+    table_row = jnp.pad(table_grad.reshape(1, -1), ((0, 0), (0, width - table_grad.size)))
+    small = jnp.concatenate(
+        [gain_attn_grad[None], gain_moe_grad[None], table_row, router_grad], axis=0
+    )
+    totals = jnp.sum(lax.all_gather(small, ("expert", "shard")), axis=0)
+    gain_attn_total, gain_moe_total = totals[0], totals[1]
+    table_total = totals[2, : table_grad.size].reshape(table_grad.shape)
+    router_total = totals[3:].T
     return (
         output,
         grad_tokens,

time: 510 us -> 461 us (0.904)
  blocking collectives: 38.8 us -> 0 us
  waiting for transfers between devices: 237 us -> 210 us
  local copies, waits for them, and re-layouts: 31.6 us -> 38.4 us
  other arithmetic: 25.5 us -> 31 us
    all_gather x1, waiting for transfers between devices: 60.5 us -> 6.6 us  [body(): totals = jnp.sum(lax.all_gather(small, ('expert', 'shard')), axis=0)]
    ppermute x20 -> x24, waiting for transfers between devices: 125 us -> 168 us  [swap(): lax.ppermute(value, axis, [(place, place ^ mask) for place in range(count)])]
    psum x1 -> x0, blocking collectives: 38.8 us -> none  [body(): lax.psum((gain_attn_grad, gain_moe_grad, table_grad, router_grad), ('expe...]
    all_to_all x1, waiting for transfers between devices: 18.5 us -> 2.82 us  [body(): lax.all_to_all(result.reshape(sources, item_count, width), 'expert', spli...]
    ppermute x20 -> x24, starting transfers between devices: 25.2 us -> 27.9 us  [swap(): lax.ppermute(value, axis, [(place, place ^ mask) for place in range(count)])]
    unnamed x79 -> x82, local copies, waits for them, and re-layouts: 9.79 us -> 12.4 us
  transfers between devices with their start and end apart: 29 -> 33, of which waited for: 16 -> 20; matrix products, arithmetic and copies ran while one was open for 24% -> 28% of each run, Pallas kernels for 5% -> 6%
where the time goes in v3:
time: 461 us; the launch traced here: 452 us
  waiting for transfers between devices  210 us (46%)
  matrix products  84.8 us (18%)
  starting transfers between devices  45.7 us (10%)
  local copies, waits for them, and re-layouts  38.4 us (8%)
  other arithmetic  31 us (7%)
  Pallas kernels  27.2 us (6%)
  between operations  15.2 us (3%)
    ppermute x24, waiting for transfers between devices, swap(): lax.ppermute(value, axis, [(place, place ^ mask) for place in range(count)])  168 us
    ppermute x24, starting transfers between devices, swap(): lax.ppermute(value, axis, [(place, place ^ mask) for place in range(count)])  27.9 us
    dot_general x7, matrix products, contract_rows(): lax.dot_general(left, right, (((0,), (0,)), ((), ())), precision=precisio...  20.7 us
    dot_general x1, matrix products, body(): jnp.dot(received.reshape(-1, width), in_full, preferred_element_type=jnp....  18.8 us
    all_to_all x1, waiting for transfers between devices, body(): lax.all_to_all(send_rows, 'expert', split_axis=0, concat_axis=0, tiled=True)  16.7 us
    pallas_call x1, Pallas kernels, attend_back(): pl.pallas_call(partial(attend_back_kernel, head_size ** (-0.5)), grid=(pa...  15.8 us
    all_to_all x1, waiting for transfers between devices, body(): lax.all_to_all(grad_back_rows.reshape(grad_received.shape), 'expert', spl...  14 us
    unnamed x82, local copies, waits for them, and re-layouts  12.4 us
  transfers between devices with their start and end apart: 33, of which 20 were waited for; matrix products, arithmetic and copies ran while one was open for 28% of the time, Pallas kernels for 6%

profile of v3, /device:TPU:0, one launch (start us, length us, event | category | flops | bytes accessed | tf_op | source)
XLA Modules:
  0.0 452.2 jit_solution(4094648148988859391)
XLA Ops:
  9.6 2.9 collective-permute-start
  14.1 12.9 %collective-permute-done = bf16[192,1536]{1,0:T(8,128)(2,1)} collective-permute-done((bf16[192,1536]{1,0:T(8,128)(2,1)}, bf16[192,1536]{1,0:T(8,128)(2,1)}, u32[]{:S(2)}, u32[]{:S(2)}) %collective-permute-start) | collective-permute-done | bytes 589856 | tf_op jit(solution)/shard_map/ppermute | solution.py:225
  28.2 12.2 %collective-permute-done.1 = bf16[192,1536]{1,0:T(8,128)(2,1)} collective-permute-done((bf16[192,1536]{1,0:T(8,128)(2,1)}, bf16[192,1536]{1,0:T(8,128)(2,1)}, u32[]{:S(2)}, u32[]{:S(2)}) %collective-permute-start.1) | collective-permute-done | bytes 589856 | tf_op jit(solution)/shard_map/ppermute | solution.py:225
  41.6 4.5 collective-permute-done.3
  56.9 3.5 convolution_convert_fusion.3.q_ref
  70.0 22.1 %collective-permute-done.4 = bf16[256,1536]{1,0:T(8,128)(2,1)} collective-permute-done((bf16[256,1536]{1,0:T(8,128)(2,1)}, bf16[256,1536]{1,0:T(8,128)(2,1)}, u32[]{:S(2)}, u32[]{:S(2)}) %collective-permute-start.4) | collective-permute-done | bytes 786464 | tf_op jit(solution)/shard_map/ppermute | solution.py:225
  94.7 31.6 %collective-permute-done.6 = bf16[256,1536]{1,0:T(8,128)(2,1)} collective-permute-done((bf16[256,1536]{1,0:T(8,128)(2,1)}, bf16[256,1536]{1,0:T(8,128)(2,1)}, u32[]{:S(2)}, u32[]{:S(2)}) %collective-permute-start.6) | collective-permute-done | bytes 786464 | tf_op jit(solution)/shard_map/ppermute | solution.py:225
  127.5 11.5 %shard_map.204 = (f32[256,768]{1,0:T(8,128)S(1)}, f32[256,768]{1,0:T(8,128)S(1)}) custom-call(bf16[256,2304]{1,0:T(8,128)(2,1)S(1)} %copy-done.2, bf16[1024,1536]{1,0:T(8,128)(2,1)S(1)} %bitcast.160, bf16[1024,1536]{1,0:T(8,128)(2,1)S(1)} %bitcast.161, f32[12,8,1280]{2,1,0:T(8,128)S(1)} %copy-done.7, s32[256,1]{1,0:T(8,128)S(1)} %copy.86.segq_ref, ...), custom_call_target="tpu_custom_call" | custom-call | flops 1610612736 | bytes 5111808 | tf_op jit(solution)/shard_map/pallas_call | solution.py:174
  144.2 4.6 %all-to-all-start = ((bf16[8,64,768]{2,1,0:T(8,128)(2,1)}), bf16[8,64,768]{2,1,0:T(8,128)(2,1)}, u32[]{:S(2)}, u32[]{:S(2)}) async-start(bf16[8,64,768]{2,1,0:T(8,128)(2,1)} %bitcast.171), calls=%async_computation | async-start | bytes 1572864 | tf_op jit(solution)/shard_map/all_to_all | solution.py:358
  153.2 16.7 %all-to-all-done = bf16[8,64,768]{2,1,0:T(8,128)(2,1)} async-done(((bf16[8,64,768]{2,1,0:T(8,128)(2,1)}), bf16[8,64,768]{2,1,0:T(8,128)(2,1)}, u32[]{:S(2)}, u32[]{:S(2)}) %all-to-all-start) | async-done | bytes 786464 | tf_op jit(solution)/shard_map/all_to_all | solution.py:358
  169.9 4.2 all-to-all-start.1
  174.4 18.8 %multiply_convert_fusion = (bf16[512,3072]{1,0:T(8,128)(2,1)}, f32[512,3072]{1,0:T(8,128)}, f32[512,3072]{1,0:T(8,128)}) fusion(bf16[512,768]{1,0:T(8,128)(2,1)} %bitcast.29, bf16[768,3072]{1,0:T(8,128)(2,1)} %all-gather.6.cloned.1.call-done), kind=kOutput, calls=%fused_computation.3 | convolution fusion | flops 2518155264 | bytes 21233664 | tf_op jit(solution)/shard_map/dot_general | solution.py:375
  195.1 6.9 %convolution_convert_fusion.2 = bf16[3072,768]{1,0:T(8,128)(2,1)} fusion(bf16[512,3072]{1,0:T(8,128)(2,1)} %get-tuple-element.82, bf16[512,768]{1,0:T(8,128)(2,1)} %bitcast.31), kind=kOutput, calls=%fused_computation.19 | convolution fusion | flops 2418278400 | bytes 8650752 | tf_op jit(solution)/shard_map/dot_general | solution.py:32
  202.1 6.8 %convolution_convert_fusion.6 = bf16[512,768]{1,0:T(8,128)(2,1)} fusion(bf16[512,3072]{1,0:T(8,128)(2,1)} %get-tuple-element.82, bf16[3072,768]{1,0:T(8,128)(2,1)} %all-gather.8.cloned.1.call-done), kind=kOutput, calls=%fused_computation.43 | convolution fusion | flops 2416312320 | bytes 8650752 | tf_op jit(solution)/shard_map/dot_general | solution.py:381
  208.9 4.4 all-to-all-start.2
  213.3 10.6 %add_convert_fusion = bf16[512,3072]{1,0:T(8,128)(2,1)S(1)} fusion(f32[512,3072]{1,0:T(8,128)} %get-tuple-element.83, f32[512,3072]{1,0:T(8,128)} %get-tuple-element.116, bf16[512,768]{1,0:T(8,128)(2,1)} %bitcast.31, bf16[3072,768]{1,0:T(8,128)(2,1)} %all-gather.8.cloned.1.call-done), kind=kOutput, calls=%fused_computation.2 | convolution fusion | flops 2437939200 | bytes 21233664 | tf_op jit(solution)/shard_map/dot_general | solution.py:394
  225.5 5.9 %convolution_convert_fusion.5 = bf16[512,768]{1,0:T(8,128)(2,1)} fusion(bf16[512,3072]{1,0:T(8,128)(2,1)S(1)} %add_convert_fusion, bf16[768,3072]{1,0:T(8,128)(2,1)} %all-gather.6.cloned.1.call-done), kind=kOutput, calls=%fused_computation.42 | convolution fusion | flops 2416312320 | bytes 8650752 | tf_op jit(solution)/shard_map/dot_general | solution.py:398
  234.3 4.2 all-to-all-start.3
  238.5 7.0 %convolution_convert_fusion.1 = bf16[768,3072]{1,0:T(8,128)(2,1)} fusion(bf16[512,768]{1,0:T(8,128)(2,1)} %bitcast.29, bf16[512,3072]{1,0:T(8,128)(2,1)} %copy-done.38), kind=kOutput, calls=%fused_computation.18 | convolution fusion | flops 2418278400 | bytes 8650752 | tf_op jit(solution)/shard_map/dot_general | solution.py:32
  245.5 14.0 %all-to-all-done.3 = bf16[8,64,768]{2,1,0:T(8,128)(2,1)} async-done(((bf16[8,64,768]{2,1,0:T(8,128)(2,1)}), bf16[8,64,768]{2,1,0:T(8,128)(2,1)}, u32[]{:S(2)}, u32[]{:S(2)}) %all-to-all-start.3) | async-done | bytes 786464 | tf_op jit(solution)/shard_map/all_to_all | solution.py:402
  275.3 15.8 %shard_map.205 = (bf16[256,768]{1,0:T(8,128)(2,1)S(1)}, bf16[1024,1536]{1,0:T(8,128)(2,1)S(1)}, f32[12,8,1280]{2,1,0:T(8,128)S(1)}) custom-call(bf16[256,2304]{1,0:T(8,128)(2,1)S(1)} %copy-done.3, bf16[1024,1536]{1,0:T(8,128)(2,1)S(1)} %bitcast.162, bf16[1024,1536]{1,0:T(8,128)(2,1)S(1)} %bitcast.163, f32[12,8,1280]{2,1,0:T(8,128)S(1)} %copy-done.8, ...), custom_call_target="tpu_custom_call" | custom-call | flops 4026531840 | bytes 9043968 | tf_op jit(solution)/shard_map/pallas_call | solution.py:194
  305.3 23.2 %collective-permute-done.10 = bf16[256,1536]{0,1:T(8,128)(2,1)} collective-permute-done((bf16[256,1536]{0,1:T(8,128)(2,1)}, bf16[256,1536]{0,1:T(8,128)(2,1)}, u32[]{:S(2)}, u32[]{:S(2)}) %collective-permute-start.10) | collective-permute-done | bytes 786464 | tf_op jit(solution)/shard_map/ppermute | solution.py:225
  328.5 18.5 %collective-permute-done.11 = bf16[256,1536]{0,1:T(8,128)(2,1)} collective-permute-done((bf16[256,1536]{0,1:T(8,128)(2,1)}, bf16[256,1536]{0,1:T(8,128)(2,1)}, u32[]{:S(2)}, u32[]{:S(2)}) %collective-permute-start.11) | collective-permute-done | bytes 786464 | tf_op jit(solution)/shard_map/ppermute | solution.py:225
  350.7 2.8 pad_maximum_fusion.1
  353.5 4.2 broadcast_select_fusion
  362.6 4.0 add_convert_fusion.1
  372.0 4.5 fusion.27
  377.2 7.2 %collective-permute-done.14 = bf16[192,1536]{1,0:T(8,128)(2,1)} collective-permute-done((bf16[192,1536]{1,0:T(8,128)(2,1)}, bf16[192,1536]{1,0:T(8,128)(2,1)}, u32[]{:S(2)}, u32[]{:S(2)}) %collective-permute-start.14) | collective-permute-done | bytes 589856 | tf_op jit(solution)/shard_map/ppermute | solution.py:225
  384.4 13.1 %collective-permute-done.15 = bf16[192,1536]{1,0:T(8,128)(2,1)} collective-permute-done((bf16[192,1536]{1,0:T(8,128)(2,1)}, bf16[192,1536]{1,0:T(8,128)(2,1)}, u32[]{:S(2)}, u32[]{:S(2)}) %collective-permute-start.15) | collective-permute-done | bytes 589856 | tf_op jit(solution)/shard_map/ppermute | solution.py:225
  405.8 7.1 %collective-permute-done.18 = bf16[48,1536]{1,0:T(8,128)(2,1)S(1)} collective-permute-done((bf16[48,1536]{1,0:T(8,128)(2,1)S(1)}, bf16[48,1536]{1,0:T(8,128)(2,1)S(1)}, u32[]{:S(2)}, u32[]{:S(2)}) %collective-permute-start.18) | collective-permute-done | bytes 147488 | tf_op jit(solution)/shard_map/ppermute | solution.py:225
  420.0 10.7 %collective-permute-done.21 = bf16[48,1536]{1,0:T(8,128)(2,1)S(1)} collective-permute-done((bf16[48,1536]{1,0:T(8,128)(2,1)S(1)}, bf16[48,1536]{1,0:T(8,128)(2,1)S(1)}, u32[]{:S(2)}, u32[]{:S(2)}) %collective-permute-start.21) | collective-permute-done | bytes 147488 | tf_op jit(solution)/shard_map/ppermute | solution.py:225
  432.5 6.6 %all-gather.10.cloned.1.call-done = f32[32,11,768]{2,1,0:T(8,128)} async-done(((f32[1,11,768]{2,1,0:T(8,128)}), f32[32,11,768]{2,1,0:T(8,128)}) %all-gather.10.cloned.1.call-update) | async-done | bytes 1081360 | tf_op jit(solution)/shard_map/all_gather | solution.py:456
  (261 shorter events, 114.0 us)
Async XLA Ops:
  7.2 167.2 %all-gather.6.cloned.1.call-start = ((), (), s32[]{:S(2)}) async-start(), calls=%async_computation.6 | async-start | bytes 5898240 | tf_op jit(solution)/shard_map/all_gather | solution.py:313
  9.6 17.4 %collective-permute-start = (bf16[192,1536]{1,0:T(8,128)(2,1)}, bf16[192,1536]{1,0:T(8,128)(2,1)}, u32[]{:S(2)}, u32[]{:S(2)}) collective-permute-start(bf16[192,1536]{1,0:T(8,128)(2,1)} %get-tuple-element.85), channel_id=1, source_target_pairs={{0,1},{1,0},{2,3},{3,2},{4,5},{5,4},{6,7},{7,6},{8,9},{9,8},{10,11... | collective-permute-start | bytes 1769480 | tf_op jit(solution)/shard_map/ppermute | solution.py:225
  12.6 27.7 %collective-permute-start.1 = (bf16[192,1536]{1,0:T(8,128)(2,1)}, bf16[192,1536]{1,0:T(8,128)(2,1)}, u32[]{:S(2)}, u32[]{:S(2)}) collective-permute-start(bf16[192,1536]{1,0:T(8,128)(2,1)} %get-tuple-element.85), channel_id=1, source_target_pairs={{0,2},{1,3},{2,0},{3,1},{4,6},{5,7},{6,4},{7,5},{8,10},{9,11},{10,... | collective-permute-start | bytes 1769480 | tf_op jit(solution)/shard_map/ppermute | solution.py:225
  14.1 27.3 %collective-permute-start.2 = (bf16[192,1536]{1,0:T(8,128)(2,1)}, bf16[192,1536]{1,0:T(8,128)(2,1)S(1)}, u32[]{:S(2)}, u32[]{:S(2)}) collective-permute-start(bf16[192,1536]{1,0:T(8,128)(2,1)} %get-tuple-element.85), channel_id=1, source_target_pairs={{0,3},{1,2},{2,1},{3,0},{4,7},{5,6},{6,5},{7,4},{8,11},{9,10},{10,... | collective-permute-start | bytes 1769480 | tf_op jit(solution)/shard_map/ppermute | solution.py:225
  49.3 152.7 %all-gather.8.cloned.1.call-start = ((), (), s32[]{:S(2)}) async-start(), calls=%async_computation.7 | async-start | bytes 5898240 | tf_op jit(solution)/shard_map/all_gather | solution.py:314
  49.4 15.4 %collective-permute-start.7 = (s32[256]{0:T(256)S(1)}, s32[256]{0:T(256)S(1)}, u32[]{:S(2)}, u32[]{:S(2)}) collective-permute-start(s32[256]{0:T(256)S(1)} %copy-done.36), channel_id=1, source_target_pairs={{0,1},{1,0},{2,3},{3,2},{4,5},{5,4},{6,7},{7,6},{8,9},{9,8},{10,11... | collective-permute-start | bytes 3080 | tf_op jit(solution)/shard_map/ppermute | solution.py:225
  49.5 15.3 %collective-permute-start.8 = (s32[256]{0:T(256)S(1)}, s32[256]{0:T(256)S(1)}, u32[]{:S(2)}, u32[]{:S(2)}) collective-permute-start(s32[256]{0:T(256)S(1)} %copy-done.36), channel_id=1, source_target_pairs={{0,2},{1,3},{2,0},{3,1},{4,6},{5,7},{6,4},{7,5},{8,10},{9,11},{10,... | collective-permute-start | bytes 3080 | tf_op jit(solution)/shard_map/ppermute | solution.py:225
  51.5 13.3 %collective-permute-start.9 = (s32[256]{0:T(256)S(1)}, s32[256]{0:T(256)S(1)}, u32[]{:S(2)}, u32[]{:S(2)}) collective-permute-start(s32[256]{0:T(256)S(1)} %copy-done.36), channel_id=1, source_target_pairs={{0,3},{1,2},{2,1},{3,0},{4,7},{5,6},{6,5},{7,4},{8,11},{9,10},{10,... | collective-permute-start | bytes 3080 | tf_op jit(solution)/shard_map/ppermute | solution.py:225
  62.4 29.7 %collective-permute-start.4 = (bf16[256,1536]{1,0:T(8,128)(2,1)}, bf16[256,1536]{1,0:T(8,128)(2,1)}, u32[]{:S(2)}, u32[]{:S(2)}) collective-permute-start(bf16[256,1536]{1,0:T(8,128)(2,1)} %slice.232), channel_id=1, source_target_pairs={{0,1},{1,0},{2,3},{3,2},{4,5},{5,4},{6,7},{7,6},{8,9},{9,8},{10,11... | collective-permute-start | bytes 2359304 | tf_op jit(solution)/shard_map/ppermute | solution.py:225
  64.9 28.6 %collective-permute-start.5 = (bf16[256,1536]{1,0:T(8,128)(2,1)}, bf16[256,1536]{1,0:T(8,128)(2,1)}, u32[]{:S(2)}, u32[]{:S(2)}) collective-permute-start(bf16[256,1536]{1,0:T(8,128)(2,1)} %slice.232), channel_id=1, source_target_pairs={{0,2},{1,3},{2,0},{3,1},{4,6},{5,7},{6,4},{7,5},{8,10},{9,11},{10,... | collective-permute-start | bytes 2359304 | tf_op jit(solution)/shard_map/ppermute | solution.py:225
  67.1 59.2 %collective-permute-start.6 = (bf16[256,1536]{1,0:T(8,128)(2,1)}, bf16[256,1536]{1,0:T(8,128)(2,1)}, u32[]{:S(2)}, u32[]{:S(2)}) collective-permute-start(bf16[256,1536]{1,0:T(8,128)(2,1)} %slice.232), channel_id=1, source_target_pairs={{0,3},{1,2},{2,1},{3,0},{4,7},{5,6},{6,5},{7,4},{8,11},{9,10},{10,... | collective-permute-start | bytes 2359304 | tf_op jit(solution)/shard_map/ppermute | solution.py:225
  144.2 25.7 %all-to-all-start = ((bf16[8,64,768]{2,1,0:T(8,128)(2,1)}), bf16[8,64,768]{2,1,0:T(8,128)(2,1)}, u32[]{:S(2)}, u32[]{:S(2)}) async-start(bf16[8,64,768]{2,1,0:T(8,128)(2,1)} %bitcast.171), calls=%async_computation | async-start | bytes 1572864 | tf_op jit(solution)/shard_map/all_to_all | solution.py:358
  169.9 25.2 %all-to-all-start.1 = ((bf16[8,64,768]{2,1,0:T(8,128)(2,1)}), bf16[8,64,768]{2,1,0:T(8,128)(2,1)}, u32[]{:S(2)}, u32[]{:S(2)}) async-start(bf16[8,64,768]{2,1,0:T(8,128)(2,1)} %bitcast.170), calls=%async_computation.1 | async-start | bytes 1572864 | tf_op jit(solution)/shard_map/all_to_all | solution.py:367
  174.1 95.5 %reduce-scatter.3.cloned.1.call-start = ((), (), s32[]{:S(2)}) async-start(), calls=%async_computation.8 | async-start | bytes 5898240 | tf_op jit(solution)/shard_map/reduce_scatter | solution.py:380
  208.9 25.4 %all-to-all-start.2 = ((bf16[8,64,768]{2,1,0:T(8,128)(2,1)}), bf16[8,64,768]{2,1,0:T(8,128)(2,1)}, u32[]{:S(2)}, u32[]{:S(2)}) async-start(bf16[8,64,768]{2,1,0:T(8,128)(2,1)} %bitcast.184), calls=%async_computation.2 | async-start | bytes 1572864 | tf_op jit(solution)/shard_map/all_to_all | solution.py:384
  234.3 25.2 %all-to-all-start.3 = ((bf16[8,64,768]{2,1,0:T(8,128)(2,1)}), bf16[8,64,768]{2,1,0:T(8,128)(2,1)}, u32[]{:S(2)}, u32[]{:S(2)}) async-start(bf16[8,64,768]{2,1,0:T(8,128)(2,1)} %bitcast.183), calls=%async_computation.3 | async-start | bytes 1572864 | tf_op jit(solution)/shard_map/all_to_all | solution.py:402
  238.5 115.1 %reduce-scatter.5.cloned.1.call-start = ((), (), s32[]{:S(2)}) async-start(), calls=%async_computation.9 | async-start | bytes 5898240 | tf_op jit(solution)/shard_map/reduce_scatter | solution.py:411
  259.5 179.6 %all-gather.10.cloned.1.call-start = ((), (), s32[]{:S(2)}) async-start(), calls=%async_computation.10 | async-start | bytes 1622016 | tf_op jit(solution)/shard_map/all_gather | solution.py:456
  295.1 33.4 %collective-permute-start.10 = (bf16[256,1536]{0,1:T(8,128)(2,1)}, bf16[256,1536]{0,1:T(8,128)(2,1)}, u32[]{:S(2)}, u32[]{:S(2)}) collective-permute-start(bf16[256,1536]{0,1:T(8,128)(2,1)} %bitcast.180), channel_id=1, source_target_pairs={{0,1},{1,0},{2,3},{3,2},{4,5},{5,4},{6,7},{7,6},{8,9},{9,8},{10,11... | collective-permute-start | bytes 2359304 | tf_op jit(solution)/shard_map/ppermute | solution.py:225
  298.6 48.5 %collective-permute-start.11 = (bf16[256,1536]{0,1:T(8,128)(2,1)}, bf16[256,1536]{0,1:T(8,128)(2,1)}, u32[]{:S(2)}, u32[]{:S(2)}) collective-permute-start(bf16[256,1536]{0,1:T(8,128)(2,1)} %bitcast.181), channel_id=1, source_target_pairs={{0,2},{1,3},{2,0},{3,1},{4,6},{5,7},{6,4},{7,5},{8,10},{9,11},{10,... | collective-permute-start | bytes 2359304 | tf_op jit(solution)/shard_map/ppermute | solution.py:225
  301.0 46.1 %collective-permute-start.12 = (bf16[256,1536]{0,1:T(8,128)(2,1)}, bf16[256,1536]{0,1:T(8,128)(2,1)}, u32[]{:S(2)}, u32[]{:S(2)}) collective-permute-start(bf16[256,1536]{0,1:T(8,128)(2,1)} %bitcast.182), channel_id=1, source_target_pairs={{0,3},{1,2},{2,1},{3,0},{4,7},{5,6},{6,5},{7,4},{8,11},{9,10},{10,... | collective-permute-start | bytes 2359304 | tf_op jit(solution)/shard_map/ppermute | solution.py:225
  357.7 4.9 %collective-permute-start.13 = (bf16[768,1536]{1,0:T(8,128)(2,1)}, bf16[768,1536]{1,0:T(8,128)(2,1)}, u32[]{:S(2)}, u32[]{:S(2)}) collective-permute-start(bf16[768,1536]{1,0:T(8,128)(2,1)} %broadcast_select_fusion), channel_id=1, source_target_pairs={{0,4},{4,0},{8,12},{12,8},{16,20},{20,16},{24,28},{28,24},{1,5},{5... | collective-permute-start | bytes 7077896 | tf_op jit(solution)/shard_map/ppermute | solution.py:225
  367.9 16.5 %collective-permute-start.14 = (bf16[192,1536]{1,0:T(8,128)(2,1)}, bf16[192,1536]{1,0:T(8,128)(2,1)}, u32[]{:S(2)}, u32[]{:S(2)}) collective-permute-start(bf16[192,1536]{1,0:T(8,128)(2,1)} %get-tuple-element.92), channel_id=1, source_target_pairs={{0,1},{1,0},{2,3},{3,2},{4,5},{5,4},{6,7},{7,6},{8,9},{9,8},{10,11... | collective-permute-start | bytes 1769480 | tf_op jit(solution)/shard_map/ppermute | solution.py:225
  369.0 28.4 %collective-permute-start.15 = (bf16[192,1536]{1,0:T(8,128)(2,1)}, bf16[192,1536]{1,0:T(8,128)(2,1)}, u32[]{:S(2)}, u32[]{:S(2)}) collective-permute-start(bf16[192,1536]{1,0:T(8,128)(2,1)} %get-tuple-element.94), channel_id=1, source_target_pairs={{0,2},{1,3},{2,0},{3,1},{4,6},{5,7},{6,4},{7,5},{8,10},{9,11},{10,... | collective-permute-start | bytes 1769480 | tf_op jit(solution)/shard_map/ppermute | solution.py:225
  369.7 27.7 %collective-permute-start.16 = (bf16[192,1536]{1,0:T(8,128)(2,1)}, bf16[192,1536]{1,0:T(8,128)(2,1)}, u32[]{:S(2)}, u32[]{:S(2)}) collective-permute-start(bf16[192,1536]{1,0:T(8,128)(2,1)} %get-tuple-element.93), channel_id=1, source_target_pairs={{0,3},{1,2},{2,1},{3,0},{4,7},{5,6},{6,5},{7,4},{8,11},{9,10},{10,... | collective-permute-start | bytes 1769480 | tf_op jit(solution)/shard_map/ppermute | solution.py:225
  399.2 6.6 %collective-permute-start.17 = (bf16[48,1536]{1,0:T(8,128)(2,1)S(1)}, bf16[48,1536]{1,0:T(8,128)(2,1)S(1)}, u32[]{:S(2)}, u32[]{:S(2)}) collective-permute-start(bf16[48,1536]{1,0:T(8,128)(2,1)S(1)} %get-tuple-element.105), channel_id=1, source_target_pairs={{0,8},{4,12},{8,0},{12,4},{16,24},{20,28},{24,16},{28,20},{1,9},{5... | collective-permute-start | bytes 442376 | tf_op jit(solution)/shard_map/ppermute | solution.py:225
  399.3 13.7 %collective-permute-start.18 = (bf16[48,1536]{1,0:T(8,128)(2,1)S(1)}, bf16[48,1536]{1,0:T(8,128)(2,1)S(1)}, u32[]{:S(2)}, u32[]{:S(2)}) collective-permute-start(bf16[48,1536]{1,0:T(8,128)(2,1)S(1)} %get-tuple-element.107), channel_id=1, source_target_pairs={{0,16},{4,20},{8,24},{12,28},{16,0},{20,4},{24,8},{28,12},{1,17},{... | collective-permute-start | bytes 442376 | tf_op jit(solution)/shard_map/ppermute | solution.py:225
  401.6 11.4 %collective-permute-start.19 = (bf16[48,1536]{1,0:T(8,128)(2,1)S(1)}, bf16[48,1536]{1,0:T(8,128)(2,1)S(1)}, u32[]{:S(2)}, u32[]{:S(2)}) collective-permute-start(bf16[48,1536]{1,0:T(8,128)(2,1)S(1)} %get-tuple-element.106), channel_id=1, source_target_pairs={{0,24},{4,28},{8,16},{12,20},{16,8},{20,12},{24,0},{28,4},{1,25},{... | collective-permute-start | bytes 442376 | tf_op jit(solution)/shard_map/ppermute | solution.py:225
  413.1 6.9 %collective-permute-start.20 = (bf16[48,1536]{1,0:T(8,128)(2,1)S(1)}, bf16[48,1536]{1,0:T(8,128)(2,1)S(1)}, u32[]{:S(2)}, u32[]{:S(2)}) collective-permute-start(bf16[48,1536]{1,0:T(8,128)(2,1)S(1)} %get-tuple-element.81), channel_id=1, source_target_pairs={{0,8},{4,12},{8,0},{12,4},{16,24},{20,28},{24,16},{28,20},{1,9},{5... | collective-permute-start | bytes 442376 | tf_op jit(solution)/shard_map/ppermute | solution.py:225
  416.6 14.1 %collective-permute-start.21 = (bf16[48,1536]{1,0:T(8,128)(2,1)S(1)}, bf16[48,1536]{1,0:T(8,128)(2,1)S(1)}, u32[]{:S(2)}, u32[]{:S(2)}) collective-permute-start(bf16[48,1536]{1,0:T(8,128)(2,1)S(1)} %get-tuple-element.81), channel_id=1, source_target_pairs={{0,16},{4,20},{8,24},{12,28},{16,0},{20,4},{24,8},{28,12},{1,17},{... | collective-permute-start | bytes 442376 | tf_op jit(solution)/shard_map/ppermute | solution.py:225
  416.9 13.8 %collective-permute-start.22 = (bf16[48,1536]{1,0:T(8,128)(2,1)S(1)}, bf16[48,1536]{1,0:T(8,128)(2,1)S(1)}, u32[]{:S(2)}, u32[]{:S(2)}) collective-permute-start(bf16[48,1536]{1,0:T(8,128)(2,1)S(1)} %get-tuple-element.81), channel_id=1, source_target_pairs={{0,24},{4,28},{8,16},{12,20},{16,8},{20,12},{24,0},{28,4},{1,25},{... | collective-permute-start | bytes 442376 | tf_op jit(solution)/shard_map/ppermute | solution.py:225
  430.7 11.9 %collective-permute-start.23 = (bf16[192,1536]{1,0:T(8,128)(2,1)S(1)}, bf16[192,1536]{1,0:T(8,128)(2,1)S(1)}, u32[]{:S(2)}, u32[]{:S(2)}) collective-permute-start(bf16[192,1536]{1,0:T(8,128)(2,1)S(1)} %bitcast.175), channel_id=1, source_target_pairs={{0,4},{4,0},{8,12},{12,8},{16,20},{20,16},{24,28},{28,24},{1,5},{5... | collective-permute-start | bytes 1769480 | tf_op jit(solution)/shard_map/ppermute | solution.py:225
  (40 other events, 670.8 us)
Sparse Core Ops, SparseCore 0:
  49.5 83.4 all-gather.5
  134.8 57.0 all-gather.7
  202.2 54.7 reduce-scatter.2
  259.8 86.5 reduce-scatter.4
  377.3 61.7 all-gather.9
